TPU v7x, 128 devices: a whole 4x4x4 slice. The times are simulated.
128 devices in a mesh: lat: 8 (over z, x_hi), lon: 16 (over x_lo, y, core).
Axes of the slice: x: 4 (x_hi: 2, x_lo: 2; x = x_hi * 2 + x_lo), y: 4, z: 4, core: 2. Of those that a mesh axis runs over, the one named last changes fastest.
Arguments:
- tokens: bfloat16 [96, 2048, 384], P('lat', 'lon'), may hold values from -7 to 7
- neighbor_mask: int32 [96, 5, 3], P('lat'), may hold values from 0 to 1, as said below
- w_query: bfloat16 [384, 384], replicated
- w_key: bfloat16 [384, 384], replicated
- w_value: bfloat16 [384, 384], replicated, may hold values from -0.3125 to 0.3125
- w_out: bfloat16 [384, 384], replicated, may hold values from -0.3125 to 0.3125
Outputs:
- layer_output: bfloat16 [96, 2048, 384], P('lat', 'lon')
Inputs may be any that keep to these rules, and one draw needn't show every extreme that they name: `neighbor_mask`: entry [i, 2, 1] is 1 for every row; for the 2 rows nearest either pole every entry of column 1 is 1.
All inputs are finite; a program needn't handle non-finite values.
Results may differ from a plain program's by a relative error of at most 0.011.
Values may be sent and summed in bfloat16 or wider, within the bound.
A program may use at most 128 MiB of HBM per device.

v0:
```python
import jax
import jax.numpy as jnp
from jax import lax
from jax.sharding import PartitionSpec as P

HEADS = 8
HEAD_DIM = 48
RADIUS = 2
POLAR = 1
CAP = 3
ANTI = 1


BIG_NEG = -1e30


def padded(cells, sides, width, closed):
    for axis, dim in sides:
        count = lax.axis_size(axis)
        ends = count if closed else count - 1
        head = lax.slice_in_dim(cells, 0, width, axis=dim)
        tail = lax.slice_in_dim(cells, cells.shape[dim] - width, cells.shape[dim], axis=dim)
        cells = jnp.concatenate(
            [
                lax.ppermute(tail, axis, [(i, (i + 1) % count) for i in range(ends)]),
                cells,
                lax.ppermute(head, axis, [((i + 1) % count, i) for i in range(ends)]),
            ],
            axis=dim,
        )
    return cells


def passed_along(value, axis, steps):
    count = lax.axis_size(axis)
    pairs = [(source, (source + steps) % count) for source in range(count)]
    return lax.ppermute(value, axis, pairs)


def project(field_data, weight):
    flattened = field_data.reshape(-1, field_data.shape[-1])
    result = jnp.dot(flattened, weight, preferred_element_type=jnp.float32)
    return result.astype(jnp.bfloat16).reshape(field_data.shape[:-1] + (weight.shape[1],))


def attend(row_queries, row_keys, row_values, counts):
    query_count = row_queries.shape[0]
    head_queries = row_queries.reshape(query_count, HEADS, HEAD_DIM)
    head_keys = row_keys.reshape(-1, HEADS, HEAD_DIM)
    head_values = row_values.reshape(-1, HEADS, HEAD_DIM)
    scores = jnp.einsum(
        "qhd,khd->hqk", head_queries, head_keys, preferred_element_type=jnp.float32
    ) * HEAD_DIM ** (-0.5)
    allowed = counts > 0
    scores = jnp.where(allowed[None, None, :], scores, BIG_NEG)
    highest = jnp.max(scores, axis=-1, keepdims=True)
    unscaled = counts[None, None, :] * jnp.exp(scores - highest)
    weights = unscaled.astype(jnp.bfloat16)
    running_sum = jnp.sum(unscaled, axis=-1)
    numerator = jnp.einsum("hqk,khd->qhd", weights, head_values, preferred_element_type=jnp.float32)
    return (numerator / running_sum.T[:, :, None]).reshape(query_count, -1).astype(jnp.bfloat16)


def cap_counts(center, sign):
    offsets = jnp.arange(2 * RADIUS + 1) - RADIUS
    target = jnp.arange(POLAR)[:, None] + sign * offsets[None, :]
    target = jnp.where(target < 0, -1 - target, target)
    matches = target[:, :, None] == jnp.arange(CAP)[None, None, :]
    return jnp.sum(jnp.where(matches, center[:, :, None], 0), axis=1).astype(jnp.float32)


def absorb(carry_state, cap_queries, head_keys, head_values, key_counts):
    running_max, running_sum, numerator = carry_state
    scores = jnp.einsum(
        "pqhd,khd->phqk", cap_queries, head_keys, preferred_element_type=jnp.float32
    ) * HEAD_DIM ** (-0.5)
    allowed = key_counts[:, None, None, :] > 0
    scores = jnp.where(allowed, scores, BIG_NEG)
    new_max = jnp.maximum(running_max, jnp.max(scores, axis=-1))
    unscaled = key_counts[:, None, None, :] * jnp.exp(scores - new_max[..., None])
    weights = unscaled.astype(jnp.bfloat16)
    factor = jnp.exp(running_max - new_max)
    new_sum = running_sum * factor + jnp.sum(unscaled, axis=-1)
    added = jnp.einsum("phqk,khd->phqd", weights, head_values, preferred_element_type=jnp.float32)
    return (new_max, new_sum, numerator * factor[..., None] + added)


def splice_rows(framed, north_far, south_far, at_north, at_south, row_count):
    upper_rows = jnp.where(at_north, north_far[::-1], framed[RADIUS - ANTI : RADIUS])
    lower_rows = jnp.where(
        at_south, south_far[::-1], framed[row_count + RADIUS : row_count + RADIUS + ANTI]
    )
    return jnp.concatenate(
        [
            framed[: RADIUS - ANTI],
            upper_rows,
            framed[RADIUS : row_count + RADIUS],
            lower_rows,
            framed[row_count + RADIUS + ANTI :],
        ],
        axis=0,
    )


def per_device(tokens, neighbor_mask, w_query, w_key, w_value, w_out):
    row_count, block_len, feat_width = tokens.shape
    lat_count = lax.axis_size("lat")
    lon_count = lax.axis_size("lon")
    lat_index = lax.axis_index("lat")
    at_north = lat_index == 0
    at_south = lat_index == lat_count - 1
    queries = project(tokens, w_query)
    keyval = jnp.concatenate([project(tokens, w_key), project(tokens, w_value)], axis=-1)
    widened = padded(keyval, (("lon", 1),), block_len, True)
    north_far, south_far = passed_along(
        (widened[:ANTI], widened[row_count - ANTI :]), "lon", lon_count // 2
    )
    framed = padded(widened, (("lat", 0),), RADIUS, False)
    framed = splice_rows(framed, north_far, south_far, at_north, at_south, row_count)
    span = 2 * RADIUS + 1

    def one_row(row_index):
        window = lax.dynamic_slice_in_dim(framed, row_index, span, 0).reshape(-1, 2 * feat_width)
        mask_row = lax.dynamic_index_in_dim(neighbor_mask, row_index, 0, keepdims=False)
        counts = jnp.repeat(mask_row.reshape(-1), block_len).astype(jnp.float32)
        row_queries = lax.dynamic_index_in_dim(queries, row_index, 0, keepdims=False)
        return attend(row_queries, window[:, :feat_width], window[:, feat_width:], counts)

    attended = lax.map(one_row, jnp.arange(row_count))
    at_pole = jnp.logical_or(at_north, at_south)
    center = neighbor_mask[:, :, 1]
    cap_queries = jnp.where(at_north, queries[:POLAR], queries[row_count - POLAR :][::-1])
    cap_keyval = jnp.where(at_north, keyval[:CAP], keyval[row_count - CAP :][::-1])
    cap_count = jnp.where(
        at_north, cap_counts(center[:POLAR], 1), cap_counts(center[row_count - POLAR :][::-1], -1)
    )
    key_counts = jnp.repeat(cap_count, block_len, axis=1)
    head_queries = cap_queries.reshape(POLAR, block_len, HEADS, HEAD_DIM)
    start_state = (
        jnp.full((POLAR, HEADS, block_len), BIG_NEG, jnp.float32),
        jnp.zeros((POLAR, HEADS, block_len), jnp.float32),
        jnp.zeros((POLAR, HEADS, block_len, HEAD_DIM), jnp.float32),
    )

    def fold_piece(carry_state, shard_piece, start_at):
        sub_count = shard_piece.shape[1] // block_len
        sub_blocks = jnp.moveaxis(
            shard_piece.reshape(CAP, sub_count, block_len, 2 * feat_width), 1, 0
        )

        def absorb_block(inner_state, sub_block):
            flattened = sub_block.reshape(CAP * block_len, 2 * feat_width)
            part_keys = flattened[:, :feat_width].reshape(-1, HEADS, HEAD_DIM)
            part_values = flattened[:, feat_width:].reshape(-1, HEADS, HEAD_DIM)
            return (absorb(inner_state, head_queries, part_keys, part_values, key_counts), None)

        return lax.scan(absorb_block, carry_state, sub_blocks)[0]

    def keep_state(carry_state, shard_piece, start_at):
        return carry_state

    final_state = lax.cond(
        at_pole,
        fold_piece,
        keep_state,
        start_state,
        lax.all_gather(cap_keyval, "lon", axis=1, tiled=True),
        jnp.int32(0),
    )
    safe_sum = jnp.where(at_pole, final_state[1], 1.0)
    polar_out = (
        (final_state[2] / safe_sum[..., None])
        .transpose(0, 2, 1, 3)
        .reshape(POLAR, block_len, feat_width)
        .astype(jnp.bfloat16)
    )
    head_rows = jnp.where(at_north, polar_out, attended[:POLAR])
    tail_rows = jnp.where(at_south, polar_out[::-1], attended[row_count - POLAR :])
    attended = jnp.concatenate([head_rows, attended[POLAR : row_count - POLAR], tail_rows], axis=0)
    return project(attended, w_out)


def solution(mesh):
    placed = (P("lat", "lon", None), P("lat", None, None), P(), P(), P(), P())
    return jax.shard_map(
        per_device, mesh=mesh, in_specs=placed, out_specs=P("lat", "lon", None), check_vma=False
    )
```

profile of v0, /device:TPU:0, one launch (start us, length us, event | category | flops | bytes accessed | tf_op | source)
XLA Modules:
  0.0 542.3 jit_solution(7078750531252645747)
XLA Ops:
  10.9 3.8 collective-permute-start.1
  14.7 26.5 %collective-permute-done = bf16[12,128,768]{2,1,0:T(8,128)(2,1)S(1)} collective-permute-done((bf16[12,128,768]{2,1,0:T(8,128)(2,1)S(1)}, bf16[12,128,768]{2,1,0:T(8,128)(2,1)S(1)}, u32[]{:S(2)}, u32[]{:S(2)}) %collective-permute-start) | collective-permute-done | bytes 2359328 | tf_op jit(solution)/shard_map/ppermute | solution.py:25
  41.3 3.9 pad_maximum_fusion.1
  48.9 6.0 %collective-permute-start.2 = (bf16[2,384,768]{2,1,0:T(8,128)(2,1)}, bf16[2,384,768]{2,1,0:T(8,128)(2,1)}, u32[]{:S(2)}, u32[]{:S(2)}) collective-permute-start(bf16[2,384,768]{2,1,0:T(8,128)(2,1)} %get-tuple-element.236), channel_id=1, source_target_pairs={{0,16},{16,32},{32,48},{48,64},{64,80},{80,96},{96,112},{1,17},{17... | collective-permute-start | bytes 3538952 | tf_op jit(solution)/shard_map/ppermute | solution.py:25
  69.5 25.3 %collective-permute-done.2 = bf16[2,384,768]{2,1,0:T(8,128)(2,1)} collective-permute-done((bf16[2,384,768]{2,1,0:T(8,128)(2,1)}, bf16[2,384,768]{2,1,0:T(8,128)(2,1)}, u32[]{:S(2)}, u32[]{:S(2)}) %collective-permute-start.2) | collective-permute-done | bytes 1179680 | tf_op jit(solution)/shard_map/ppermute | solution.py:25
  96.7 23.3 %collective-permute-done.3 = bf16[1,384,768]{2,1,0:T(8,128)(2,1)} collective-permute-done((bf16[1,384,768]{2,1,0:T(8,128)(2,1)}, bf16[1,384,768]{2,1,0:T(8,128)(2,1)}, u32[]{:S(2)}, u32[]{:S(2)}) %collective-permute-start.3) | collective-permute-done | bytes 589856 | tf_op jit(solution)/shard_map/ppermute | solution.py:37
  125.6 17.7 %collective-permute-done.4 = bf16[1,384,768]{2,1,0:T(8,128)(2,1)S(1)} collective-permute-done((bf16[1,384,768]{2,1,0:T(8,128)(2,1)}, bf16[1,384,768]{2,1,0:T(8,128)(2,1)S(1)}, u32[]{:S(2)}, u32[]{:S(2)}) %collective-permute-start.4) | collective-permute-done | bytes 589856 | tf_op jit(solution)/shard_map/ppermute | solution.py:37
  143.3 21.7 %collective-permute-done.5 = bf16[2,384,768]{2,1,0:T(8,128)(2,1)S(1)} collective-permute-done((bf16[2,384,768]{2,1,0:T(8,128)(2,1)}, bf16[2,384,768]{2,1,0:T(8,128)(2,1)S(1)}, u32[]{:S(2)}, u32[]{:S(2)}) %collective-permute-start.5) | collective-permute-done | bytes 1179680 | tf_op jit(solution)/shard_map/ppermute | solution.py:27
  166.8 264.7 %while.25 = (s32[]{:T(128)}, bf16[12,128,384]{1,2,0:T(8,128)(2,1)}, s32[12]{0:T(128)S(1)}, bf16[16,384,768]{2,1,0:T(8,128)(2,1)}, s32[12,5,3]{2,1,0:T(8,128)}, /...) while((s32[]{:T(128)}, bf16[12,128,384]{1,2,0:T(8,128)(2,1)}, ...), condition=%wide.region_11.12_spmd, body=%wide.region_8.11_spmd.sunk | while | flops 389385984 | bytes 29323040 | solution.py:129
  176.9 6.2 %fusion.81 = (f32[8,128]{1,0:T(8,128)S(1)}, bf16[8,128,1920]{2,1,0:T(8,128)(2,1)}) fusion(pred[1920]{0:T(1024)(128)(4,1)S(1)} %bitcast_compare_fusion.4, bf16[128,8,48]{0,2,1:T(8,128)(2,1)S(1)} %bitcast.179, bf16[1920,8,48]{0,2,1:T(8,128)(2,1)} %bitcast.161, f32[1920]{0:T(1024)S(1)} %broadcast_bitcast_fusion.4), kind=kOutput, calls=%fused_computation.84.clone.1 | convolution fusion | flops 200542080 | bytes 5518720 | tf_op jit(solution)/shard_map/while/body/eval_jaxpr/sub | solution.py:57
  184.6 3.6 fusion.82
  199.0 6.2 %fusion.81 = (f32[8,128]{1,0:T(8,128)S(1)}, bf16[8,128,1920]{2,1,0:T(8,128)(2,1)}) fusion(pred[1920]{0:T(1024)(128)(4,1)S(1)} %bitcast_compare_fusion.4, bf16[128,8,48]{0,2,1:T(8,128)(2,1)S(1)} %bitcast.179, bf16[1920,8,48]{0,2,1:T(8,128)(2,1)} %bitcast.161, f32[1920]{0:T(1024)S(1)} %broadcast_bitcast_fusion.4), kind=kOutput, calls=%fused_computation.84.clone.1 | convolution fusion | flops 200542080 | bytes 5518720 | tf_op jit(solution)/shard_map/while/body/eval_jaxpr/sub | solution.py:57
  221.0 6.2 %fusion.81 = (f32[8,128]{1,0:T(8,128)S(1)}, bf16[8,128,1920]{2,1,0:T(8,128)(2,1)}) fusion(pred[1920]{0:T(1024)(128)(4,1)S(1)} %bitcast_compare_fusion.4, bf16[128,8,48]{0,2,1:T(8,128)(2,1)S(1)} %bitcast.179, bf16[1920,8,48]{0,2,1:T(8,128)(2,1)} %bitcast.161, f32[1920]{0:T(1024)S(1)} %broadcast_bitcast_fusion.4), kind=kOutput, calls=%fused_computation.84.clone.1 | convolution fusion | flops 200542080 | bytes 5518720 | tf_op jit(solution)/shard_map/while/body/eval_jaxpr/sub | solution.py:57
  243.1 6.2 %fusion.81 = (f32[8,128]{1,0:T(8,128)S(1)}, bf16[8,128,1920]{2,1,0:T(8,128)(2,1)}) fusion(pred[1920]{0:T(1024)(128)(4,1)S(1)} %bitcast_compare_fusion.4, bf16[128,8,48]{0,2,1:T(8,128)(2,1)S(1)} %bitcast.179, bf16[1920,8,48]{0,2,1:T(8,128)(2,1)} %bitcast.161, f32[1920]{0:T(1024)S(1)} %broadcast_bitcast_fusion.4), kind=kOutput, calls=%fused_computation.84.clone.1 | convolution fusion | flops 200542080 | bytes 5518720 | tf_op jit(solution)/shard_map/while/body/eval_jaxpr/sub | solution.py:57
  250.8 3.6 fusion.82
  265.2 6.2 %fusion.81 = (f32[8,128]{1,0:T(8,128)S(1)}, bf16[8,128,1920]{2,1,0:T(8,128)(2,1)}) fusion(pred[1920]{0:T(1024)(128)(4,1)S(1)} %bitcast_compare_fusion.4, bf16[128,8,48]{0,2,1:T(8,128)(2,1)S(1)} %bitcast.179, bf16[1920,8,48]{0,2,1:T(8,128)(2,1)} %bitcast.161, f32[1920]{0:T(1024)S(1)} %broadcast_bitcast_fusion.4), kind=kOutput, calls=%fused_computation.84.clone.1 | convolution fusion | flops 200542080 | bytes 5518720 | tf_op jit(solution)/shard_map/while/body/eval_jaxpr/sub | solution.py:57
  272.8 3.6 fusion.82
  287.2 6.2 %fusion.81 = (f32[8,128]{1,0:T(8,128)S(1)}, bf16[8,128,1920]{2,1,0:T(8,128)(2,1)}) fusion(pred[1920]{0:T(1024)(128)(4,1)S(1)} %bitcast_compare_fusion.4, bf16[128,8,48]{0,2,1:T(8,128)(2,1)S(1)} %bitcast.179, bf16[1920,8,48]{0,2,1:T(8,128)(2,1)} %bitcast.161, f32[1920]{0:T(1024)S(1)} %broadcast_bitcast_fusion.4), kind=kOutput, calls=%fused_computation.84.clone.1 | convolution fusion | flops 200542080 | bytes 5518720 | tf_op jit(solution)/shard_map/while/body/eval_jaxpr/sub | solution.py:57
  294.8 3.6 fusion.82
  309.3 6.2 %fusion.81 = (f32[8,128]{1,0:T(8,128)S(1)}, bf16[8,128,1920]{2,1,0:T(8,128)(2,1)}) fusion(pred[1920]{0:T(1024)(128)(4,1)S(1)} %bitcast_compare_fusion.4, bf16[128,8,48]{0,2,1:T(8,128)(2,1)S(1)} %bitcast.179, bf16[1920,8,48]{0,2,1:T(8,128)(2,1)} %bitcast.161, f32[1920]{0:T(1024)S(1)} %broadcast_bitcast_fusion.4), kind=kOutput, calls=%fused_computation.84.clone.1 | convolution fusion | flops 200542080 | bytes 5518720 | tf_op jit(solution)/shard_map/while/body/eval_jaxpr/sub | solution.py:57
  316.9 3.6 fusion.82
  331.3 6.2 %fusion.81 = (f32[8,128]{1,0:T(8,128)S(1)}, bf16[8,128,1920]{2,1,0:T(8,128)(2,1)}) fusion(pred[1920]{0:T(1024)(128)(4,1)S(1)} %bitcast_compare_fusion.4, bf16[128,8,48]{0,2,1:T(8,128)(2,1)S(1)} %bitcast.179, bf16[1920,8,48]{0,2,1:T(8,128)(2,1)} %bitcast.161, f32[1920]{0:T(1024)S(1)} %broadcast_bitcast_fusion.4), kind=kOutput, calls=%fused_computation.84.clone.1 | convolution fusion | flops 200542080 | bytes 5518720 | tf_op jit(solution)/shard_map/while/body/eval_jaxpr/sub | solution.py:57
  353.4 6.2 %fusion.81 = (f32[8,128]{1,0:T(8,128)S(1)}, bf16[8,128,1920]{2,1,0:T(8,128)(2,1)}) fusion(pred[1920]{0:T(1024)(128)(4,1)S(1)} %bitcast_compare_fusion.4, bf16[128,8,48]{0,2,1:T(8,128)(2,1)S(1)} %bitcast.179, bf16[1920,8,48]{0,2,1:T(8,128)(2,1)} %bitcast.161, f32[1920]{0:T(1024)S(1)} %broadcast_bitcast_fusion.4), kind=kOutput, calls=%fused_computation.84.clone.1 | convolution fusion | flops 200542080 | bytes 5518720 | tf_op jit(solution)/shard_map/while/body/eval_jaxpr/sub | solution.py:57
  361.0 3.6 fusion.82
  375.4 6.2 %fusion.81 = (f32[8,128]{1,0:T(8,128)S(1)}, bf16[8,128,1920]{2,1,0:T(8,128)(2,1)}) fusion(pred[1920]{0:T(1024)(128)(4,1)S(1)} %bitcast_compare_fusion.4, bf16[128,8,48]{0,2,1:T(8,128)(2,1)S(1)} %bitcast.179, bf16[1920,8,48]{0,2,1:T(8,128)(2,1)} %bitcast.161, f32[1920]{0:T(1024)S(1)} %broadcast_bitcast_fusion.4), kind=kOutput, calls=%fused_computation.84.clone.1 | convolution fusion | flops 200542080 | bytes 5518720 | tf_op jit(solution)/shard_map/while/body/eval_jaxpr/sub | solution.py:57
  383.1 3.6 fusion.82
  397.5 6.2 %fusion.81 = (f32[8,128]{1,0:T(8,128)S(1)}, bf16[8,128,1920]{2,1,0:T(8,128)(2,1)}) fusion(pred[1920]{0:T(1024)(128)(4,1)S(1)} %bitcast_compare_fusion.4, bf16[128,8,48]{0,2,1:T(8,128)(2,1)S(1)} %bitcast.179, bf16[1920,8,48]{0,2,1:T(8,128)(2,1)} %bitcast.161, f32[1920]{0:T(1024)S(1)} %broadcast_bitcast_fusion.4), kind=kOutput, calls=%fused_computation.84.clone.1 | convolution fusion | flops 200542080 | bytes 5518720 | tf_op jit(solution)/shard_map/while/body/eval_jaxpr/sub | solution.py:57
  405.1 3.6 fusion.82
  419.5 6.2 %fusion.81 = (f32[8,128]{1,0:T(8,128)S(1)}, bf16[8,128,1920]{2,1,0:T(8,128)(2,1)}) fusion(pred[1920]{0:T(1024)(128)(4,1)S(1)} %bitcast_compare_fusion.4, bf16[128,8,48]{0,2,1:T(8,128)(2,1)S(1)} %bitcast.179, bf16[1920,8,48]{0,2,1:T(8,128)(2,1)} %bitcast.161, f32[1920]{0:T(1024)S(1)} %broadcast_bitcast_fusion.4), kind=kOutput, calls=%fused_computation.84.clone.1 | convolution fusion | flops 200542080 | bytes 5518720 | tf_op jit(solution)/shard_map/while/body/eval_jaxpr/sub | solution.py:57
  427.2 3.6 fusion.82
  434.9 95.5 %conditional.1 = (f32[1,8,128]{2,1,0:T(8,128)}, f32[1,8,128,48]{2,3,1,0:T(8,128)}) conditional(s32[]{:T(128)} %convert_element_type.80, () %tuple.21, (bf16[3,2048,768]{2,1,0:T(8,128)(2,1)}, pred[]{:T(512)}, bf16[1536,384]{1,0:T(8,128)(2,1)S(1)}, f32[3]{0:T(128)S(1)}, f32[3]{0:T(128)S(1)}) %tuple.87), branch_computations={%region_2.3_spmd, %region_3.8_spmd} | conditional | flops 79239552 | bytes 12064267 | solution.py:162
  437.4 93.0 %while.24 = (s32[]{:T(128)}, f32[1,8,128]{2,1,0:T(8,128)S(1)}, f32[1,8,128]{2,1,0:T(8,128)}, f32[1,8,128,48]{2,3,1,0:T(8,128)}, bf16[16,3,128,768]{3,2,0,1:T(8,1...) while((s32[]{:T(128)}, f32[1,8,128]{2,1,0:T(8,128)S(1)}, ...), condition=%wide.region_7.7_spmd.clone, body=%wide.region_4.6_spmd.clone.sunk | while | flops 79190400 | bytes 9409925 | solution.py:157
  (411 shorter events, 254.8 us)
Async XLA Ops:
  6.5 1.3 copy-start
  6.5 426.7 %all-gather.2.cloned.1.call-start = ((), (), s32[]{:S(2)}) async-start(), calls=%async_computation | async-start | bytes 10027008 | tf_op jit(solution)/shard_map/all_gather | solution.py:167
  7.8 1.9 copy-start.10
  10.8 34.4 %copy-start.6 = (bf16[12,128,768]{2,1,0:T(8,128)(2,1)}, bf16[12,128,768]{2,1,0:T(8,128)(2,1)S(1)}, u32[]{:S(2)}) copy-start(bf16[12,128,768]{2,1,0:T(8,128)(2,1)S(1)} %pad_maximum_fusion.4) | copy-start | bytes 7077892
  10.8 30.4 %collective-permute-start = (bf16[12,128,768]{2,1,0:T(8,128)(2,1)S(1)}, bf16[12,128,768]{2,1,0:T(8,128)(2,1)S(1)}, u32[]{:S(2)}, u32[]{:S(2)}) collective-permute-start(bf16[12,128,768]{2,1,0:T(8,128)(2,1)S(1)} %pad_maximum_fusion.4), channel_id=1, source_target_pairs={{0,1},{1,2},{2,3},{3,4},{4,5},{5,6},{6,7},{7,8},{8,9},{9,10},{10,1... | collective-permute-start | bytes 7077896 | tf_op jit(solution)/shard_map/ppermute | solution.py:25
  10.9 30.4 %collective-permute-start.1 = (bf16[12,128,768]{2,1,0:T(8,128)(2,1)S(1)}, bf16[12,128,768]{2,1,0:T(8,128)(2,1)S(1)}, u32[]{:S(2)}, u32[]{:S(2)}) collective-permute-start(bf16[12,128,768]{2,1,0:T(8,128)(2,1)S(1)} %pad_maximum_fusion.4), channel_id=1, source_target_pairs={{1,0},{2,1},{3,2},{4,3},{5,4},{6,5},{7,6},{8,7},{9,8},{10,9},{11,1... | collective-permute-start | bytes 7077896 | tf_op jit(solution)/shard_map/ppermute | solution.py:27
  41.3 3.9 copy-start.2
  41.3 4.4 copy-start.4
  48.9 45.9 %collective-permute-start.2 = (bf16[2,384,768]{2,1,0:T(8,128)(2,1)}, bf16[2,384,768]{2,1,0:T(8,128)(2,1)}, u32[]{:S(2)}, u32[]{:S(2)}) collective-permute-start(bf16[2,384,768]{2,1,0:T(8,128)(2,1)} %get-tuple-element.236), channel_id=1, source_target_pairs={{0,16},{16,32},{32,48},{48,64},{64,80},{80,96},{96,112},{1,17},{17... | collective-permute-start | bytes 3538952 | tf_op jit(solution)/shard_map/ppermute | solution.py:25
  55.8 2.1 copy-start.12
  58.3 64.0 %copy-start.7 = (bf16[12,128,768]{2,1,0:T(8,128)(2,1)S(1)}, bf16[12,128,768]{2,1,0:T(8,128)(2,1)}, u32[]{:S(2)}) copy-start(bf16[12,128,768]{2,1,0:T(8,128)(2,1)} %copy-done.6) | copy-start | bytes 7077892
  60.8 59.3 %collective-permute-start.3 = (bf16[1,384,768]{2,1,0:T(8,128)(2,1)}, bf16[1,384,768]{2,1,0:T(8,128)(2,1)}, u32[]{:S(2)}, u32[]{:S(2)}) collective-permute-start(bf16[1,384,768]{2,1,0:T(8,128)(2,1)} %get-tuple-element.238), channel_id=1, source_target_pairs={{0,8},{1,9},{2,10},{3,11},{4,12},{5,13},{6,14},{7,15},{8,0},{9,1},... | collective-permute-start | bytes 1769480 | tf_op jit(solution)/shard_map/ppermute | solution.py:37
  63.6 58.7 %copy-start.5 = (bf16[12,128,768]{2,1,0:T(8,128)(2,1)S(1)}, bf16[12,128,768]{2,1,0:T(8,128)(2,1)}, u32[]{:S(2)}) copy-start(bf16[12,128,768]{2,1,0:T(8,128)(2,1)} %copy-done.4) | copy-start | bytes 7077892
  66.6 55.7 %copy-start.3 = (bf16[12,128,768]{2,1,0:T(8,128)(2,1)S(1)}, bf16[12,128,768]{2,1,0:T(8,128)(2,1)}, u32[]{:S(2)}) copy-start(bf16[12,128,768]{2,1,0:T(8,128)(2,1)} %copy-done.2) | copy-start | bytes 7077892
  66.6 98.4 %collective-permute-start.5 = (bf16[2,384,768]{2,1,0:T(8,128)(2,1)}, bf16[2,384,768]{2,1,0:T(8,128)(2,1)S(1)}, u32[]{:S(2)}, u32[]{:S(2)}) collective-permute-start(bf16[2,384,768]{2,1,0:T(8,128)(2,1)} %get-tuple-element.235), channel_id=1, source_target_pairs={{16,0},{32,16},{48,32},{64,48},{80,64},{96,80},{112,96},{17,1},{33... | collective-permute-start | bytes 3538952 | tf_op jit(solution)/shard_map/ppermute | solution.py:27
  68.0 75.3 %collective-permute-start.4 = (bf16[1,384,768]{2,1,0:T(8,128)(2,1)}, bf16[1,384,768]{2,1,0:T(8,128)(2,1)S(1)}, u32[]{:S(2)}, u32[]{:S(2)}) collective-permute-start(bf16[1,384,768]{2,1,0:T(8,128)(2,1)} %get-tuple-element.237), channel_id=1, source_target_pairs={{0,8},{1,9},{2,10},{3,11},{4,12},{5,13},{6,14},{7,15},{8,0},{9,1},... | collective-permute-start | bytes 1769480 | tf_op jit(solution)/shard_map/ppermute | solution.py:37
  433.2 1.7 copy-start.9
  433.2 1.7 copy-start.8
  530.4 3.0 slice-start
  532.1 1.5 copy-start.11
  533.4 2.1 copy-start.1
Sparse Core Ops, SparseCore 0:
  58.0 92.6 all-gather.1
where the time goes:
time: 547 us; the launch traced here: 542 us
  matrix products  166 us (30%)
  local copies, waits for them, and re-layouts  143 us (26%)
  waiting for transfers between devices  115 us (21%)
  other arithmetic  53.8 us (10%)
  loops' own time  38.3 us (7%)
  between operations  13.6 us (2%)
  starting transfers between devices  13.5 us (2%)
    sub x12, matrix products, attend(): unscaled = counts[None, None, :] * jnp.exp(scores - highest)  74.6 us
    ppermute x2, waiting for transfers between devices, padded(): lax.ppermute(tail, axis, [(i, (i + 1) % count) for i in range(ends)])  51.8 us
    dot_general x12, matrix products, attend(): jnp.einsum('hqk,khd->qhd', weights, head_values, preferred_element_type=j...  43.7 us
    ppermute x2, waiting for transfers between devices, passed_along(): return lax.ppermute(value, axis, pairs)  41 us
    another operation x1, loops' own time, per_device(): attended = lax.map(one_row, jnp.arange(row_count))  37.6 us
    dot_general x16, matrix products, absorb(): jnp.einsum('phqk,khd->phqd', weights, head_values, preferred_element_type...  31.3 us
    slice x24, local copies, waits for them, and re-layouts, one_row(): window[:, :feat_width]  29.2 us
    dynamic_slice x12, local copies, waits for them, and re-layouts, one_row(): lax.dynamic_slice_in_dim(framed, row_index, span, 0)  24.3 us
  transfers between devices with their start and end apart: 7, of which 5 were waited for; matrix products, arithmetic and copies ran while one was open for 46% of the time, Pallas kernels for 0%

commit v1 on v0

v1 whole, which is shorter than its diff:
```python
import functools

import jax
import jax.numpy as jnp
from jax import lax
from jax.experimental import pallas as pl
from jax.experimental.pallas import tpu as pltpu
from jax.sharding import PartitionSpec as P

HEADS = 8
HEAD_DIM = 48
PAIRS = 4
WIDTH = 384
BLOCK = 128
ROWS = 12
RADIUS = 2
SPAN = 5
FRAME = ROWS + 2 * RADIUS
DUMMY = 3 * FRAME
VROWS = 112
LANES = 128 * PAIRS
GROUP = 8
AHEAD = 8
SCORE_SCALE = HEAD_DIM ** -0.5 * 1.4426950408889634
SUM_LOW = 1e-30
SUM_HIGH = 1e30
VMEM_LIMIT = 56 * 2**20
F32 = jnp.float32
BF16 = jnp.bfloat16
VMEM_SPEC = pl.BlockSpec(memory_space=pltpu.VMEM)
SMEM_SPEC = pl.BlockSpec(memory_space=pltpu.SMEM)
ANY_SPEC = pl.BlockSpec(memory_space=pl.ANY)


def dot(a, b, dims=((1,), (0,))):
    return lax.dot_general(a, b, (dims, ((), ())), preferred_element_type=F32)


def prepare_keys(w_key_ref, wide_ref):
    wide_ref[...] = jnp.zeros_like(wide_ref)
    for p in range(PAIRS):
        wide_ref[:, 128 * p : 128 * p + 96] = w_key_ref[:, 96 * p : 96 * p + 96]


def flipped(ref):
    return ref[...].astype(F32).T.astype(BF16)


def put_keys_values(tokens, slots, wide_ref, value_t_ref, k_ref, vt_ref):
    keys = dot(tokens, wide_ref[...]).astype(BF16)
    values = dot(value_t_ref[...], tokens, ((1,), (1,))).astype(BF16)
    for n, slot in enumerate(slots):
        k_ref[slot] = keys[128 * n : 128 * n + 128]
        for p in range(PAIRS):
            vt_ref[slot, p, 0:96] = values[96 * p : 96 * p + 96, 128 * n : 128 * n + 128]


def put_queries(tokens, rows, query_t_ref, qd_ref):
    queries = dot(query_t_ref[...], tokens, ((1,), (1,))).astype(BF16)
    for n, row in enumerate(rows):
        for p in range(PAIRS):
            part = queries[96 * p : 96 * p + 96, 128 * n : 128 * n + 128]
            qd_ref[row, p, 0:48, 0:128] = part[0:48]
            qd_ref[row, p, 48:96, 128:256] = part[48:96]


def clear_slots(k_ref, vt_ref, dummy):
    ones = jnp.ones((VROWS - 96, 128), BF16)

    def body(slot, carry):
        for p in range(PAIRS):
            vt_ref[slot, p, 96:VROWS] = ones
        return carry

    lax.fori_loop(0, vt_ref.shape[0], body, 0)
    if dummy is not None:
        k_ref[dummy] = jnp.zeros(k_ref.shape[1:], BF16)
        vt_ref[dummy] = jnp.zeros(vt_ref.shape[1:], BF16)


def run_tiles(tiles, count, q_of, k_ref, vt_ref, qd_ref, acc_ref):
    chunks = [(u, p) for u in range(count) for p in range(PAIRS)]

    def scores(chunk):
        u, p = chunk
        keys = jnp.concatenate([k_ref[s, :, 128 * p : 128 * p + 128] for s in tiles[u]], axis=0)
        return dot(keys, qd_ref[q_of[u], p])

    def values(chunk, weights):
        u, p = chunk
        return dot(jnp.concatenate([vt_ref[s, p] for s in tiles[u]], axis=1), weights)

    held = {}
    for step in range(len(chunks) + AHEAD):
        if step < len(chunks):
            held[step] = scores(chunks[step])
        if step >= AHEAD:
            chunk = chunks[step - AHEAD]
            weights = jnp.exp2(held.pop(step - AHEAD) * SCORE_SCALE).astype(BF16)
            acc_ref[q_of[chunk[0]], chunk[1]] += values(chunk, weights)


def build_lists(mask_ref, wanted, list_ref, row_ref, begin_ref, keep_of):
    pos = jnp.int32(0)
    for i in range(ROWS):
        begin_ref[2 * i] = pos
        keep = keep_of(i)
        for d in range(SPAN):
            for e in range(3):
                if not wanted(i, d, e):
                    continue
                list_ref[pos] = e * FRAME + i + d
                row_ref[pos] = i
                bit = (mask_ref[i, d, e] > 0).astype(jnp.int32)
                pos = pos + (bit if keep is None else bit * keep)
        begin_ref[2 * i + 1] = pos
        list_ref[pos] = DUMMY
        row_ref[pos] = i
        pos = (pos + 1) // 2 * 2
    for n in range(2 * GROUP):
        list_ref[pos + n] = DUMMY
        row_ref[pos + n] = 0
    return (pos + 2 * GROUP - 1) // (2 * GROUP)


def fast_rows(steps, list_ref, row_ref, k_ref, vt_ref, qd_ref, acc_ref):
    def step(t, carry):
        at = t * (2 * GROUP)
        tiles = [(list_ref[at + 2 * u], list_ref[at + 2 * u + 1]) for u in range(GROUP)]
        q_of = [row_ref[at + 2 * u] for u in range(GROUP)]
        run_tiles(tiles, GROUP, q_of, k_ref, vt_ref, qd_ref, acc_ref)
        return carry

    lax.fori_loop(0, steps, step, 0)


def safe_row(q, acc_at, begin, end, slot_of, k_ref, vt_ref, qd_ref, acc_ref, top_ref):
    top_ref[...] = jnp.full(top_ref.shape, -jnp.inf, F32)

    def scores(n, p):
        return dot(k_ref[slot_of(n), :, 128 * p : 128 * p + 128], qd_ref[q, p]) * SCORE_SCALE

    def find_top(n, carry):
        for p in range(PAIRS):
            top_ref[p] = jnp.maximum(top_ref[p], jnp.max(scores(n, p), axis=0, keepdims=True))
        return carry

    lax.fori_loop(begin, end, find_top, 0)
    acc_ref[acc_at] = jnp.zeros(acc_ref.shape[1:], F32)

    def add(n, carry):
        for p in range(PAIRS):
            weights = jnp.exp2(scores(n, p) - top_ref[p, 0:1]).astype(BF16)
            acc_ref[acc_at, p] += dot(vt_ref[slot_of(n), p], weights)
        return carry

    lax.fori_loop(begin, end, add, 0)


def sums_hold(sums):
    return jnp.where((sums >= SUM_LOW) & (sums <= SUM_HIGH), 1.0, 0.0)


def normalised(acc_ref, row):
    parts = []
    for p in range(PAIRS):
        sums = 1.0 / acc_ref[row, p, 96:97, :]
        parts.append(acc_ref[row, p, 0:48, 0:128] * sums[:, 0:128])
        parts.append(acc_ref[row, p, 48:96, 128:256] * sums[:, 128:256])
    return jnp.concatenate(parts, axis=0).astype(BF16)


def own_slot(n):
    return FRAME + RADIUS + n


def own_kernel(
    mask_ref, tokens_ref, w_query_ref, w_key_ref, w_value_ref,
    k_out, vt_out, qd_out, first_out, second_out, sums_out,
    k_ref, vt_ref, qd_ref, acc_ref, wide_ref, query_t_ref, value_t_ref, list_ref, row_ref, begin_ref, sem,
):
    prepare_keys(w_key_ref, wide_ref)
    query_t_ref[...] = flipped(w_query_ref)
    value_t_ref[...] = flipped(w_value_ref)
    clear_slots(k_ref, vt_ref, ROWS)
    qd_ref[...] = jnp.zeros_like(qd_ref)
    acc_ref[...] = jnp.zeros_like(acc_ref)

    def load(t, carry):
        tokens = tokens_ref[pl.ds(2 * t, 2)].reshape(2 * BLOCK, WIDTH)
        rows = (2 * t, 2 * t + 1)
        put_keys_values(tokens, rows, wide_ref, value_t_ref, k_ref, vt_ref)
        put_queries(tokens, rows, query_t_ref, qd_ref)
        return carry

    lax.fori_loop(0, ROWS // 2, load, 0)
    copies = [
        pltpu.make_async_copy(k_ref.at[pl.ds(0, ROWS)], k_out, sem.at[0]),
        pltpu.make_async_copy(vt_ref.at[pl.ds(0, ROWS)], vt_out, sem.at[1]),
        pltpu.make_async_copy(qd_ref, qd_out, sem.at[2]),
    ]
    for copy in copies:
        copy.start()
    pos = jnp.int32(0)
    for i in range(ROWS):
        for d in range(SPAN):
            r = i + d - RADIUS
            if not 0 <= r < ROWS:
                continue
            list_ref[pos] = r
            row_ref[pos] = i
            pos = pos + (mask_ref[i, d, 1] > 0).astype(jnp.int32)
        list_ref[pos] = ROWS
        row_ref[pos] = i
        pos = (pos + 1) // 2 * 2
    for n in range(2 * GROUP):
        list_ref[pos + n] = ROWS
        row_ref[pos + n] = 0
    steps = (pos + 2 * GROUP - 1) // (2 * GROUP)
    fast_rows(steps, list_ref, row_ref, k_ref, vt_ref, qd_ref, acc_ref)
    tail = [
        pltpu.make_async_copy(acc_ref.at[:, :, pl.ds(0, 48), pl.ds(0, 128)], first_out, sem.at[3]),
        pltpu.make_async_copy(acc_ref.at[:, :, pl.ds(48, 48), pl.ds(128, 128)], second_out, sem.at[4]),
        pltpu.make_async_copy(acc_ref.at[:, :, pl.ds(96, 8)], sums_out, sem.at[5]),
    ]
    for copy in tail:
        copy.start()
    for copy in copies + tail:
        copy.wait()


def frame_kernel(
    mask_ref, west_ref, east_ref, halo_ref, west_halo_ref, east_halo_ref,
    w_key_ref, w_value_ref, w_out_ref, own_k, own_vt, own_qd, first_in, second_in, sums_in,
    out_ref,
    k_ref, vt_ref, qd_ref, acc_ref, top_ref, hold_ref, wide_ref, value_t_ref, list_ref, row_ref, begin_ref, sem,
):
    lat = lax.axis_index("lat")
    last = lax.axis_size("lat") - 1
    own = pl.ds(own_slot(0), ROWS)
    copies = [
        pltpu.make_async_copy(own_qd, qd_ref, sem.at[2]),
        pltpu.make_async_copy(first_in, acc_ref.at[:, :, pl.ds(0, 48), pl.ds(0, 128)], sem.at[3]),
        pltpu.make_async_copy(second_in, acc_ref.at[:, :, pl.ds(48, 48), pl.ds(128, 128)], sem.at[4]),
        pltpu.make_async_copy(sums_in, acc_ref.at[:, :, pl.ds(96, 8)], sem.at[5]),
    ]
    for copy in copies:
        copy.start()
    prepare_keys(w_key_ref, wide_ref)
    value_t_ref[...] = flipped(w_value_ref)
    clear_slots(k_ref, vt_ref, DUMMY)

    def take(tokens, slots):
        put_keys_values(tokens.reshape(2 * BLOCK, WIDTH), slots, wide_ref, value_t_ref, k_ref, vt_ref)

    def load(t, carry):
        for column, ref in ((0, west_ref), (2, east_ref)):
            slot = column * FRAME + RADIUS + 2 * t
            take(ref[pl.ds(2 * t, 2)], (slot, slot + 1))
        return carry

    lax.fori_loop(0, ROWS // 2, load, 0)
    for column, ref in ((0, west_halo_ref), (1, halo_ref), (2, east_halo_ref)):
        for n, row in ((0, 0), (2, ROWS + RADIUS)):
            slot = column * FRAME + row
            take(ref[n : n + 2], (slot, slot + 1))

    def keep_of(i):
        if i == 0:
            return (lat != 0).astype(jnp.int32)
        if i == ROWS - 1:
            return (lat != last).astype(jnp.int32)
        return None

    def inside(i, d, e):
        return e == 1 and 0 <= i + d - RADIUS < ROWS

    steps = build_lists(mask_ref, lambda i, d, e: not inside(i, d, e), list_ref, row_ref, begin_ref, keep_of)
    for copy in copies:
        copy.wait()
    fast_rows(steps, list_ref, row_ref, k_ref, vt_ref, qd_ref, acc_ref)

    def finish(t, carry):
        mixed = jnp.concatenate([normalised(acc_ref, 2 * t), normalised(acc_ref, 2 * t + 1)], axis=1)
        result = dot(mixed, w_out_ref[...], ((0,), (0,))).astype(BF16)
        out_ref[pl.ds(2 * t, 2)] = result.reshape(2, BLOCK, WIDTH)
        return carry

    lax.fori_loop(0, ROWS // 2, finish, 0)
    hold_ref[...] = jnp.ones_like(hold_ref)
    for i in range(ROWS):
        for p in range(PAIRS):
            hold_ref[0:1] = jnp.minimum(hold_ref[0:1], sums_hold(acc_ref[i, p, 96:97, :]))
    holds = jnp.min(hold_ref[...]) > 0.5

    @pl.when(jnp.logical_not(holds))
    def _():
        more = [
            pltpu.make_async_copy(own_k, k_ref.at[own], sem.at[0]),
            pltpu.make_async_copy(own_vt, vt_ref.at[own], sem.at[1]),
        ]
        for copy in more:
            copy.start()
        for copy in more:
            copy.wait()
        build_lists(mask_ref, lambda i, d, e: True, list_ref, row_ref, begin_ref, lambda i: None)

        def again(i, carry):
            safe_row(
                i, i, begin_ref[2 * i], begin_ref[2 * i + 1], lambda n: list_ref[n],
                k_ref, vt_ref, qd_ref, acc_ref, top_ref,
            )
            return carry

        lax.fori_loop(0, ROWS, again, 0)
        lax.fori_loop(0, ROWS // 2, finish, 0)


def cap_kernel(
    query_tokens_ref, tokens_ref, w_query_ref, w_key_ref, w_value_ref, out_ref,
    k_ref, vt_ref, qd_ref, acc_ref, top_ref, hold_ref, wide_ref, query_t_ref, value_t_ref,
):
    lat = lax.axis_index("lat")
    last = lax.axis_size("lat") - 1
    blocks = tokens_ref.shape[0] // BLOCK

    def give(shift):
        for p in range(PAIRS):
            out_ref[96 * p : 96 * p + 48] = acc_ref[0, p, 0:48, 0:128]
            out_ref[96 * p + 48 : 96 * p + 96] = acc_ref[0, p, 48:96, 128:256]
            for half in range(2):
                lanes = slice(128 * half, 128 * half + 128)
                n = 2 * p + half
                out_ref[WIDTH + n : WIDTH + n + 1] = acc_ref[0, p, 96:97, lanes]
                out_ref[WIDTH + HEADS + n : WIDTH + HEADS + n + 1] = shift(p)[:, lanes]

    @pl.when(jnp.logical_and(lat != 0, lat != last))
    def _():
        prepare_keys(w_key_ref, wide_ref)
        query_t_ref[...] = flipped(w_query_ref)
        value_t_ref[...] = flipped(w_value_ref)
        clear_slots(k_ref, vt_ref, None)
        qd_ref[...] = jnp.zeros_like(qd_ref)
        acc_ref[...] = jnp.zeros_like(acc_ref)
        put_queries(query_tokens_ref[...], (0,), query_t_ref, qd_ref)

        def load(t, carry):
            tokens = tokens_ref[pl.ds(pl.multiple_of(t * 2 * BLOCK, 2 * BLOCK), 2 * BLOCK)]
            put_keys_values(tokens, (2 * t, 2 * t + 1), wide_ref, value_t_ref, k_ref, vt_ref)
            return carry

        lax.fori_loop(0, blocks // 2, load, 0)
        tiles = [(2 * t, 2 * t + 1) for t in range(blocks // 2)]
        run_tiles(tiles, blocks // 2, [0] * (blocks // 2), k_ref, vt_ref, qd_ref, acc_ref)
        give(lambda p: jnp.zeros((1, 256), F32))
        hold_ref[...] = jnp.ones_like(hold_ref)
        for p in range(PAIRS):
            hold_ref[0:1] = jnp.minimum(hold_ref[0:1], sums_hold(acc_ref[0, p, 96:97, :]))
        holds = jnp.min(hold_ref[...]) > 0.5

        @pl.when(jnp.logical_not(holds))
        def _():
            safe_row(0, 0, 0, blocks, lambda n: n, k_ref, vt_ref, qd_ref, acc_ref, top_ref)
            give(lambda p: top_ref[p, 0:1])


def join_kernel(mask_ref, a_ref, b_ref, c_ref, w_out_ref, layer_ref, out_ref, row_ref, sem):
    lat = lax.axis_index("lat")
    last = lax.axis_size("lat") - 1

    @pl.when(jnp.logical_or(lat == 0, lat == last))
    def _():
        row = jnp.where(lat == 0, 0, ROWS - 1)
        counts = [0, 0, 0]
        for d in range(SPAN):
            north = d - RADIUS if d >= RADIUS else RADIUS - 1 - d
            south = RADIUS - d if d <= RADIUS else d - RADIUS - 1
            bit = (mask_ref[row, d, 1] > 0).astype(jnp.int32)
            for r in range(3):
                hit = jnp.where(lat == 0, jnp.int32(north == r), jnp.int32(south == r))
                counts[r] = counts[r] + bit * hit
        parts = (a_ref, b_ref, c_ref)
        shifts = [ref[WIDTH + HEADS : WIDTH + 2 * HEADS] for ref in parts]
        low = [jnp.where(n > 0, s, -jnp.inf) for n, s in zip(counts, shifts)]
        top = jnp.maximum(jnp.maximum(low[0], low[1]), low[2])
        factors = [jnp.where(n > 0, jnp.exp2(s - top), 0.0) * n.astype(F32) for n, s in zip(counts, low)]
        total = sum(f * ref[WIDTH : WIDTH + HEADS] for f, ref in zip(factors, parts))
        heads = []
        for h in range(HEADS):
            rows = slice(HEAD_DIM * h, HEAD_DIM * h + HEAD_DIM)
            mixed = sum(f[h : h + 1] * ref[rows] for f, ref in zip(factors, parts))
            heads.append(mixed / total[h : h + 1])
        mixed = jnp.concatenate(heads, axis=0).astype(BF16)
        row_ref[...] = dot(mixed, w_out_ref[...], ((0,), (0,))).astype(BF16)
        copy = pltpu.make_async_copy(row_ref, out_ref.at[row], sem)
        copy.start()
        copy.wait()


def per_device(tokens, neighbor_mask, w_query, w_key, w_value, w_out):
    lat_count = lax.axis_size("lat")
    lon_count = lax.axis_size("lon")
    lat = lax.axis_index("lat")
    at_north = lat == 0
    at_south = lat == lat_count - 1
    last = lat_count - 1
    params = pltpu.CompilerParams(vmem_limit_bytes=VMEM_LIMIT)
    eastward = [(j, (j + 1) % lon_count) for j in range(lon_count)]
    westward = [((j + 1) % lon_count, j) for j in range(lon_count)]

    west = lax.ppermute(tokens, "lon", eastward)
    east = lax.ppermute(tokens, "lon", westward)
    north = lax.ppermute(tokens[ROWS - RADIUS :], "lat", [(i, i + 1) for i in range(last)])
    south = lax.ppermute(tokens[:RADIUS], "lat", [(i + 1, i) for i in range(last)])
    pole_row = jnp.where(at_north, tokens[:1], tokens[ROWS - 1 :])
    half = lon_count // 2
    far = lax.ppermute(pole_row, "lon", [(j, (j + half) % lon_count) for j in range(lon_count)])
    cap = jnp.where(at_north, tokens[:3], tokens[ROWS - 3 :][::-1])
    given = []
    for r in range(3):
        rows = cap[:1] if r == 0 else jnp.concatenate([cap[:1], cap[r : r + 1]], axis=0)
        given.append(lax.ppermute(rows, "lat", [(0, 1 + r), (last, last - 1 - r)]))
    helper = jnp.minimum(lat, last - lat)
    query_tokens = given[0][0] + given[1][0] + given[2][0]
    key_tokens = given[0][0] + given[1][1] + given[2][1]
    cap_tokens = lax.all_gather(key_tokens, "lon", axis=0, tiled=True)
    halo = jnp.concatenate(
        [
            north[:1],
            jnp.where(at_north, far, north[1:]),
            jnp.where(at_south, far, south[:1]),
            south[1:],
        ],
        axis=0,
    )
    west_halo = lax.ppermute(halo, "lon", eastward)
    east_halo = lax.ppermute(halo, "lon", westward)

    lists = [pltpu.SMEM((272,), jnp.int32), pltpu.SMEM((272,), jnp.int32), pltpu.SMEM((2 * ROWS,), jnp.int32)]
    k_shape = lambda n: (n, BLOCK, LANES)
    vt_shape = lambda n: (n, PAIRS, VROWS, BLOCK)
    qd_shape = lambda n: (n, PAIRS, 128, 256)
    acc_shape = lambda n: (n, PAIRS, VROWS, 256)
    square = pltpu.VMEM((WIDTH, WIDTH), BF16)
    wide = pltpu.VMEM((WIDTH, LANES), BF16)
    own = pl.pallas_call(
        own_kernel,
        out_shape=[
            jax.ShapeDtypeStruct(k_shape(ROWS), BF16),
            jax.ShapeDtypeStruct(vt_shape(ROWS), BF16),
            jax.ShapeDtypeStruct(qd_shape(ROWS), BF16),
            jax.ShapeDtypeStruct((ROWS, PAIRS, 48, 128), F32),
            jax.ShapeDtypeStruct((ROWS, PAIRS, 48, 128), F32),
            jax.ShapeDtypeStruct((ROWS, PAIRS, 8, 256), F32),
        ],
        in_specs=[SMEM_SPEC] + [VMEM_SPEC] * 4,
        out_specs=[ANY_SPEC] * 6,
        scratch_shapes=[
            pltpu.VMEM(k_shape(ROWS + 1), BF16),
            pltpu.VMEM(vt_shape(ROWS + 1), BF16),
            pltpu.VMEM(qd_shape(ROWS), BF16),
            pltpu.VMEM(acc_shape(ROWS), F32),
            wide, square, square, *lists,
            pltpu.SemaphoreType.DMA((6,)),
        ],
        compiler_params=params,
        cost_estimate=pl.CostEstimate(flops=8 * 10**9, bytes_accessed=12 * 2**20, transcendentals=0),
        name="own_column",
    )(neighbor_mask, tokens, w_query, w_key, w_value)
    capped = pl.pallas_call(
        cap_kernel,
        out_shape=jax.ShapeDtypeStruct((WIDTH + 2 * HEADS, BLOCK), F32),
        in_specs=[VMEM_SPEC] * 5,
        out_specs=VMEM_SPEC,
        scratch_shapes=[
            pltpu.VMEM(k_shape(lon_count), BF16),
            pltpu.VMEM(vt_shape(lon_count), BF16),
            pltpu.VMEM(qd_shape(1), BF16),
            pltpu.VMEM(acc_shape(1), F32),
            pltpu.VMEM((PAIRS, 8, 256), F32),
            pltpu.VMEM((8, 256), F32),
            wide, square, square,
        ],
        compiler_params=params,
        cost_estimate=pl.CostEstimate(flops=4 * 10**9, bytes_accessed=3 * 2**20, transcendentals=0),
        name="cap_rows",
    )(query_tokens, cap_tokens, w_query, w_key, w_value)
    returned = [
        lax.ppermute(capped, "lat", [(1 + r, 0), (last - 1 - r, last)]) for r in range(3)
    ]
    layer = pl.pallas_call(
        frame_kernel,
        out_shape=jax.ShapeDtypeStruct((ROWS, BLOCK, WIDTH), BF16),
        in_specs=[SMEM_SPEC] + [VMEM_SPEC] * 8 + [ANY_SPEC] * 6,
        out_specs=VMEM_SPEC,
        scratch_shapes=[
            pltpu.VMEM(k_shape(DUMMY + 1), BF16),
            pltpu.VMEM(vt_shape(DUMMY + 1), BF16),
            pltpu.VMEM(qd_shape(ROWS), BF16),
            pltpu.VMEM(acc_shape(ROWS), F32),
            pltpu.VMEM((PAIRS, 8, 256), F32),
            pltpu.VMEM((8, 256), F32),
            wide, square, *lists,
            pltpu.SemaphoreType.DMA((6,)),
        ],
        compiler_params=params,
        cost_estimate=pl.CostEstimate(flops=12 * 10**9, bytes_accessed=16 * 2**20, transcendentals=0),
        name="frame_columns",
    )(neighbor_mask, west, east, halo, west_halo, east_halo, w_key, w_value, w_out, *own)
    return pl.pallas_call(
        join_kernel,
        out_shape=jax.ShapeDtypeStruct((ROWS, BLOCK, WIDTH), BF16),
        in_specs=[SMEM_SPEC] + [VMEM_SPEC] * 4 + [ANY_SPEC],
        out_specs=ANY_SPEC,
        scratch_shapes=[pltpu.VMEM((BLOCK, WIDTH), BF16), pltpu.SemaphoreType.DMA],
        input_output_aliases={5: 0},
        compiler_params=params,
        name="join_cap",
    )(neighbor_mask, *returned, w_out, layer)


def solution(mesh):
    placed = (P("lat", "lon", None), P("lat", None, None), P(), P(), P(), P())
    return jax.shard_map(
        per_device, mesh=mesh, in_specs=placed, out_specs=P("lat", "lon", None), check_vma=False
    )
```

time: 547 us -> 247 us (0.45)
  the two profiles are of different devices: /device:TPU:0 before, /device:TPU:28 now
where the time goes in v1:
time: 247 us; the launch traced here: 246 us
  Pallas kernels  188 us (76%)
  waiting for transfers between devices  19.3 us (8%)
  starting transfers between devices  18.5 us (7%)
  between operations  13.7 us (6%)
  local copies, waits for them, and re-layouts  4.29 us (2%)
    pallas_call x1, Pallas kernels, per_device(): pl.pallas_call(frame_kernel, out_shape=jax.ShapeDtypeStruct((ROWS, BLOCK,...  146 us
    pallas_call x1, Pallas kernels, per_device(): pl.pallas_call(cap_kernel, out_shape=jax.ShapeDtypeStruct((WIDTH + 2 * HE...  25.9 us
    pallas_call x1, Pallas kernels, per_device(): pl.pallas_call(own_kernel, out_shape=[jax.ShapeDtypeStruct(k_shape(ROWS),...  14.5 us
    ppermute x3, waiting for transfers between devices, per_device(): given.append(lax.ppermute(rows, 'lat', [(0, 1 + r), (last, last - 1 - r)]))  10.8 us
    ppermute x1, waiting for transfers between devices, per_device(): lax.ppermute(pole_row, 'lon', [(j, (j + half) % lon_count) for j in range...  8.46 us
    ppermute x1, starting transfers between devices, per_device(): lax.ppermute(tokens[ROWS - RADIUS:], 'lat', [(i, i + 1) for i in range(la...  6.33 us
  transfers between devices with their start and end apart: 14, of which 2 were waited for; matrix products, arithmetic and copies ran while one was open for 0% of the time, Pallas kernels for 76%

profile of v1, /device:TPU:28, one launch (start us, length us, event | category | flops | bytes accessed | tf_op | source)
XLA Modules:
  0.0 246.1 jit_solution(16829331083807820365)
XLA Ops:
  6.5 1.0 slice.53
  7.5 1.0 reverse_select_fusion
  8.6 0.0 copy-start
  8.7 0.0 copy-start.5
  8.7 0.8 collective-permute-start.2
  9.5 0.7 collective-permute-start.1
  10.2 1.3 collective-permute-start
  11.5 10.8 %collective-permute-done = bf16[1,128,384]{2,1,0:T(8,128)(2,1)S(1)} collective-permute-done((bf16[1,128,384]{2,1,0:T(8,128)(2,1)S(1)}, bf16[1,128,384]{2,1,0:T(8,128)(2,1)S(1)}, u32[]{:S(2)}, u32[]{:S(2)}) %collective-permute-start) | collective-permute-done | bytes 98336 | tf_op jit(solution)/shard_map/ppermute | solution.py:422
  22.3 0.0 collective-permute-done.2
  22.3 0.7 slice_add_fusion
  23.0 0.0 all-gather.3.cloned.1.call-update
  23.1 1.9 collective-permute-start.10
  25.0 6.3 %collective-permute-start.8 = (bf16[2,128,384]{2,1,0:T(8,128)(2,1)S(1)}, bf16[2,128,384]{2,1,0:T(8,128)(2,1)S(1)}, u32[]{:S(2)}, u32[]{:S(2)}) collective-permute-start(bf16[2,128,384]{2,1,0:T(8,128)(2,1)S(1)} %get-tuple-element.17), channel_id=1, source_target_pairs={{0,16},{16,32},{32,48},{48,64},{64,80},{80,96},{96,112},{1,17},{17... | collective-permute-start | bytes 589832 | tf_op jit(solution)/shard_map/ppermute | solution.py:413
  31.4 1.3 collective-permute-start.9
  32.7 1.7 collective-permute-start.7
  34.4 0.7 copy.10.mask_ref
  35.1 8.5 %collective-permute-done.9 = bf16[1,128,384]{2,1,0:T(8,128)(2,1)S(1)} collective-permute-done((bf16[1,128,384]{2,1,0:T(8,128)(2,1)S(1)}, bf16[1,128,384]{2,1,0:T(8,128)(2,1)S(1)}, u32[]{:S(2)}, u32[]{:S(2)}) %collective-permute-start.9) | collective-permute-done | bytes 98336 | tf_op jit(solution)/shard_map/ppermute | solution.py:417
  43.7 0.1 pad_maximum_fusion.halo_ref
  43.7 0.1 collective-permute-start.11
  43.8 1.7 collective-permute-start.12
  45.6 14.5 %own_column.1 = (bf16[12,128,512]{2,1,0:T(8,128)(2,1)}, bf16[12,4,112,128]{3,2,1,0:T(8,128)(2,1)}, bf16[12,4,128,256]{3,2,1,0:T(8,128)(2,1)}, f32[12,4,48,128]{3...) custom-call(s32[12,5,3]{2,1,0:T(8,128)} %copy.10.mask_ref, bf16[12,128,384]{2,1,0:T(8,128)(2,1)} %tokens_ref.1, ...), custom_call_target="tpu_custom_call" | custom-call | flops 8000000000 | bytes 12582912 | tf_op jit(solution)/shard_map/own_column/pallas_call | solution.py:446
  60.1 0.0 all-gather.3.cloned.1.call-done
  60.1 25.9 %cap_rows.1 = f32[400,128]{1,0:T(8,128)} custom-call(bf16[128,384]{1,0:T(8,128)(2,1)} %get-tuple-element.20.query_tokens_ref, bf16[2048,384]{1,0:T(8,128)(2,1)} %bitcast.3, bf16[384,384]{1,0:T(8,128)(2,1)} %w_query_ref.3, bf16[384,384]{1,0:T(8,128)(2,1)} %w_key_ref.5, bf16[384,384]{1,0:T(8,128)(2,1)} %w_value_ref.5), custom_call_target="tpu_custom_call" | custom-call | flops 4000000000 | bytes 3145728 | tf_op jit(solution)/shard_map/cap_rows/pallas_call | solution.py:470
  86.0 1.3 collective-permute-start.3
  87.3 0.7 collective-permute-start.4
  88.0 0.7 collective-permute-start.5
  88.7 1.0 copy-done.6
  89.7 146.4 %frame_columns.1.layer_ref = bf16[12,128,384]{2,1,0:T(8,128)(2,1)} custom-call(s32[12,5,3]{2,1,0:T(8,128)} %copy.10.mask_ref, bf16[12,128,384]{2,1,0:T(8,128)(2,1)} %copy-done.6, bf16[12,128,384]{2,1,0:T(8,128)(2,1)} %collective-permute-done.7.east_ref, bf16[4,128,384]{2,1,0:T(8,128)(2,1)} %copy-done.1, bf16[4,128,384]{2,1,0:T(8,128)(2,1)} %copy-done.7, ...), custom_call_target="tpu_custom_call" | custom-call | flops 12000000000 | bytes 16777216 | tf_op jit(solution)/shard_map/frame_columns/pallas_call | solution.py:491
  236.1 0.7 copy-done.2
  236.8 0.1 copy-done.3
  236.9 0.7 copy-done.4
  237.6 1.6 join_cap.1
  (28 shorter events, 0.2 us)
Async XLA Ops:
  6.5 53.6 %all-gather.3.cloned.1.call-start = ((), (), s32[]{:S(2)}) async-start(), calls=%async_computation | async-start | bytes 1671168 | tf_op jit(solution)/shard_map/all_gather | solution.py:426
  8.6 14.5 %copy-start = (bf16[12,128,384]{2,1,0:T(8,128)(2,1)S(1)}, bf16[12,128,384]{2,1,0:T(8,128)(2,1)}, u32[]{:S(2)}) copy-start(bf16[12,128,384]{2,1,0:T(8,128)(2,1)} %tokens_ref.1) | copy-start | bytes 3538948
  8.7 25.7 %copy-start.5 = (s32[12,5,3]{0,2,1:T(4,128)S(1)}, s32[12,5,3]{0,2,1:T(4,128)}, u32[]{:S(2)}) copy-start(s32[12,5,3]{0,2,1:T(4,128)} %param.7) | copy-start | bytes 2164
  8.7 13.6 %collective-permute-start.2 = (bf16[2,128,384]{2,1,0:T(8,128)(2,1)S(1)}, bf16[2,128,384]{2,1,0:T(8,128)(2,1)S(1)}, u32[]{:S(2)}, u32[]{:S(2)}) collective-permute-start(bf16[2,128,384]{2,1,0:T(8,128)(2,1)S(1)} %pad_maximum_fusion.1), channel_id=1, source_target_pairs={{0,48},{112,64},{1,49},{113,65},{2,50},{114,66},{3,51},{115,67},{4... | collective-permute-start | bytes 589832 | tf_op jit(solution)/shard_map/ppermute | solution.py:422
  9.5 12.8 %collective-permute-start.1 = (bf16[2,128,384]{2,1,0:T(8,128)(2,1)S(1)}, bf16[2,128,384]{2,1,0:T(8,128)(2,1)S(1)}, u32[]{:S(2)}, u32[]{:S(2)}) collective-permute-start(bf16[2,128,384]{2,1,0:T(8,128)(2,1)S(1)} %concatenate.12), channel_id=1, source_target_pairs={{0,32},{112,80},{1,33},{113,81},{2,34},{114,82},{3,35},{115,83},{4... | collective-permute-start | bytes 589832 | tf_op jit(solution)/shard_map/ppermute | solution.py:422
  10.2 12.1 %collective-permute-start = (bf16[1,128,384]{2,1,0:T(8,128)(2,1)S(1)}, bf16[1,128,384]{2,1,0:T(8,128)(2,1)S(1)}, u32[]{:S(2)}, u32[]{:S(2)}) collective-permute-start(bf16[1,128,384]{2,1,0:T(8,128)(2,1)S(1)} %get-tuple-element.21), channel_id=1, source_target_pairs={{0,16},{112,96},{1,17},{113,97},{2,18},{114,98},{3,19},{115,99},{4... | collective-permute-start | bytes 294920 | tf_op jit(solution)/shard_map/ppermute | solution.py:422
  23.1 20.5 %collective-permute-start.10 = (bf16[2,128,384]{2,1,0:T(8,128)(2,1)S(1)}, bf16[2,128,384]{2,1,0:T(8,128)(2,1)S(1)}, u32[]{:S(2)}, u32[]{:S(2)}) collective-permute-start(bf16[2,128,384]{2,1,0:T(8,128)(2,1)S(1)} %get-tuple-element.18), channel_id=1, source_target_pairs={{16,0},{32,16},{48,32},{64,48},{80,64},{96,80},{112,96},{17,1},{33... | collective-permute-start | bytes 589832 | tf_op jit(solution)/shard_map/ppermute | solution.py:414
  25.0 18.6 %collective-permute-start.8 = (bf16[2,128,384]{2,1,0:T(8,128)(2,1)S(1)}, bf16[2,128,384]{2,1,0:T(8,128)(2,1)S(1)}, u32[]{:S(2)}, u32[]{:S(2)}) collective-permute-start(bf16[2,128,384]{2,1,0:T(8,128)(2,1)S(1)} %get-tuple-element.17), channel_id=1, source_target_pairs={{0,16},{16,32},{32,48},{48,64},{64,80},{80,96},{96,112},{1,17},{17... | collective-permute-start | bytes 589832 | tf_op jit(solution)/shard_map/ppermute | solution.py:413
  31.4 12.2 %collective-permute-start.9 = (bf16[1,128,384]{2,1,0:T(8,128)(2,1)S(1)}, bf16[1,128,384]{2,1,0:T(8,128)(2,1)S(1)}, u32[]{:S(2)}, u32[]{:S(2)}) collective-permute-start(bf16[1,128,384]{2,1,0:T(8,128)(2,1)S(1)} %slice_select_fusion.2), channel_id=1, source_target_pairs={{0,8},{1,9},{2,10},{3,11},{4,12},{5,13},{6,14},{7,15},{8,0},{9,1},... | collective-permute-start | bytes 294920 | tf_op jit(solution)/shard_map/ppermute | solution.py:417
  32.7 56.0 %collective-permute-start.6 = (bf16[12,128,384]{2,1,0:T(8,128)(2,1)S(1)}, bf16[12,128,384]{2,1,0:T(8,128)(2,1)S(1)}, u32[]{:S(2)}, u32[]{:S(2)}) collective-permute-start(bf16[12,128,384]{2,1,0:T(8,128)(2,1)S(1)} %copy-done), channel_id=1, source_target_pairs={{0,1},{1,2},{2,3},{3,4},{4,5},{5,6},{6,7},{7,8},{8,9},{9,10},{10,1... | collective-permute-start | bytes 3538952 | tf_op jit(solution)/shard_map/ppermute | solution.py:411
  32.7 56.0 %collective-permute-start.7 = (bf16[12,128,384]{2,1,0:T(8,128)(2,1)S(1)}, bf16[12,128,384]{2,1,0:T(8,128)(2,1)}, u32[]{:S(2)}, u32[]{:S(2)}) collective-permute-start(bf16[12,128,384]{2,1,0:T(8,128)(2,1)S(1)} %copy-done), channel_id=1, source_target_pairs={{1,0},{2,1},{3,2},{4,3},{5,4},{6,5},{7,6},{8,7},{9,8},{10,9},{11,1... | collective-permute-start | bytes 3538952 | tf_op jit(solution)/shard_map/ppermute | solution.py:412
  43.7 16.3 %copy-start.1 = (bf16[4,128,384]{2,1,0:T(8,128)(2,1)}, bf16[4,128,384]{2,1,0:T(8,128)(2,1)S(1)}, u32[]{:S(2)}) copy-start(bf16[4,128,384]{2,1,0:T(8,128)(2,1)S(1)} %pad_maximum_fusion.halo_ref) | copy-start | bytes 1179652
  43.7 43.5 %collective-permute-start.11 = (bf16[4,128,384]{2,1,0:T(8,128)(2,1)S(1)}, bf16[4,128,384]{2,1,0:T(8,128)(2,1)S(1)}, u32[]{:S(2)}, u32[]{:S(2)}) collective-permute-start(bf16[4,128,384]{2,1,0:T(8,128)(2,1)S(1)} %pad_maximum_fusion.halo_ref), channel_id=1, source_target_pairs={{0,1},{1,2},{2,3},{3,4},{4,5},{5,6},{6,7},{7,8},{8,9},{9,10},{10,1... | collective-permute-start | bytes 1179656 | tf_op jit(solution)/shard_map/ppermute | solution.py:436
  43.8 44.2 %collective-permute-start.12 = (bf16[4,128,384]{2,1,0:T(8,128)(2,1)S(1)}, bf16[4,128,384]{2,1,0:T(8,128)(2,1)}, u32[]{:S(2)}, u32[]{:S(2)}) collective-permute-start(bf16[4,128,384]{2,1,0:T(8,128)(2,1)S(1)} %pad_maximum_fusion.halo_ref), channel_id=1, source_target_pairs={{1,0},{2,1},{3,2},{4,3},{5,4},{6,5},{7,6},{8,7},{9,8},{10,9},{11,1... | collective-permute-start | bytes 1179656 | tf_op jit(solution)/shard_map/ppermute | solution.py:437
  86.0 150.1 %collective-permute-start.3 = (f32[400,128]{1,0:T(8,128)}, f32[400,128]{1,0:T(8,128)S(1)}, u32[]{:S(2)}, u32[]{:S(2)}) collective-permute-start(f32[400,128]{1,0:T(8,128)} %cap_rows.1), channel_id=1, source_target_pairs={{16,0},{96,112},{17,1},{97,113},{18,2},{98,114},{19,3},{99,115},{2... | collective-permute-start | bytes 614408 | tf_op jit(solution)/shard_map/ppermute | solution.py:489
  87.3 1.4 copy-start.7
  87.3 148.8 %collective-permute-start.4 = (f32[400,128]{1,0:T(8,128)}, f32[400,128]{1,0:T(8,128)S(1)}, u32[]{:S(2)}, u32[]{:S(2)}) collective-permute-start(f32[400,128]{1,0:T(8,128)} %cap_rows.1), channel_id=1, source_target_pairs={{32,0},{80,112},{33,1},{81,113},{34,2},{82,114},{35,3},{83,115},{3... | collective-permute-start | bytes 614408 | tf_op jit(solution)/shard_map/ppermute | solution.py:489
  88.0 148.2 %collective-permute-start.5 = (f32[400,128]{1,0:T(8,128)}, f32[400,128]{1,0:T(8,128)S(1)}, u32[]{:S(2)}, u32[]{:S(2)}) collective-permute-start(f32[400,128]{1,0:T(8,128)} %cap_rows.1), channel_id=1, source_target_pairs={{48,0},{64,112},{49,1},{65,113},{50,2},{66,114},{51,3},{67,115},{5... | collective-permute-start | bytes 614408 | tf_op jit(solution)/shard_map/ppermute | solution.py:489
  88.7 1.1 copy-start.6
  236.1 0.7 copy-start.2
  236.1 0.8 copy-start.3
  236.9 0.7 copy-start.4
Sparse Core Ops, SparseCore 0:
  23.1 32.6 all-gather.2

commit v2 on v1

--- a/solution.py
+++ b/solution.py
@@ -397,44 +397,172 @@
         copy.wait()
 
 
+def at_device(lat, lon):
+    return {"lat": lat, "lon": lon}
+
+
+def exchange_kernel(
+    tokens_ref, west_ref, east_ref, halo_ref, west_halo_ref, east_halo_ref, query_ref, cap_ref,
+    side_send, side_recv, halo_send, halo_recv, corner_send, corner_recv,
+    give_send, query_recv, cap_recv, ring_send, ring_recv,
+):
+    lat, lon = lax.axis_index("lat"), lax.axis_index("lon")
+    lat_count, lon_count = lax.axis_size("lat"), lax.axis_size("lon")
+    last = lat_count - 1
+    half = lon_count // 2
+    is_north, is_south = lat == 0, lat == last
+    at_pole = jnp.logical_or(is_north, is_south)
+    east_lon, west_lon = lax.rem(lon + 1, lon_count), lax.rem(lon + lon_count - 1, lon_count)
+    far_lon = lax.rem(lon + half, lon_count)
+    pole = jnp.where(lat < lat_count // 2, 0, last)
+    down = (jnp.where(is_south, lat, lat + 1), jnp.where(is_south, far_lon, lon))
+    up = (jnp.where(is_north, lat, lat - 1), jnp.where(is_north, far_lon, lon))
+
+    def send(src, dst, send_sem, recv_sem, to):
+        copy = pltpu.make_async_remote_copy(
+            src_ref=src, dst_ref=dst, send_sem=send_sem, recv_sem=recv_sem,
+            device_id=at_device(*to), device_id_type=pl.DeviceIdType.MESH,
+        )
+        copy.start()
+        return copy
+
+    barrier = pltpu.get_barrier_semaphore()
+    for to in ((lat, east_lon), (lat, west_lon), down, up):
+        pl.semaphore_signal(barrier, inc=1, device_id=at_device(*to), device_id_type=pl.DeviceIdType.MESH)
+
+    @pl.when(jnp.logical_not(at_pole))
+    def _():
+        pl.semaphore_signal(
+            barrier, inc=1, device_id=at_device(pole, lon), device_id_type=pl.DeviceIdType.MESH
+        )
+
+    @pl.when(at_pole)
+    def _():
+        pl.semaphore_wait(barrier, 7)
+
+    @pl.when(jnp.logical_not(at_pole))
+    def _():
+        pl.semaphore_wait(barrier, 4)
+
+    def cap_row(r):
+        return jnp.where(is_north, r, ROWS - 1 - r)
+
+    def helper(r):
+        return (jnp.where(is_north, 1 + r, last - 1 - r), lon)
+
+    def gifts():
+        copies = []
+        for r in range(3):
+            copies.append((tokens_ref.at[cap_row(r)], cap_ref.at[lon], give_send.at[r], cap_recv, helper(r)))
+            copies.append((tokens_ref.at[cap_row(0)], query_ref, give_send.at[3 + r], query_recv, helper(r)))
+        return copies
+
+    @pl.when(at_pole)
+    def _():
+        for gift in gifts():
+            send(*gift)
+
+    sides = []
+    for n, (row, slot, to) in enumerate(
+        (
+            (ROWS - 2, jnp.where(is_south, 3, 0), down),
+            (ROWS - 1, jnp.where(is_south, 2, 1), down),
+            (0, jnp.where(is_north, 1, 2), up),
+            (1, jnp.where(is_north, 0, 3), up),
+        )
+    ):
+        sides.append(send(tokens_ref.at[row], halo_ref.at[slot], halo_send.at[n], halo_recv.at[slot], to))
+    wide = [
+        send(tokens_ref, west_ref, side_send.at[0], side_recv.at[0], (lat, east_lon)),
+        send(tokens_ref, east_ref, side_send.at[1], side_recv.at[1], (lat, west_lon)),
+    ]
+
+    def landed(dst, sem):
+        pltpu.make_async_copy(dst, dst, sem).wait()
+
+    def ring(step, going_east):
+        if going_east:
+            block = lax.rem(lon - (step - 1) + lon_count, lon_count)
+            to, n = (lat, east_lon), 0
+        else:
+            block = lax.rem(lon + step - 1, lon_count)
+            to, n = (lat, west_lon), 1
+        return pltpu.make_async_remote_copy(
+            src_ref=cap_ref.at[block], dst_ref=cap_ref.at[block],
+            send_sem=ring_send.at[n, step - 1], recv_sem=ring_recv.at[n, step - 1],
+            device_id=at_device(*to), device_id_type=pl.DeviceIdType.MESH,
+        )
+
+    def got(step, going_east):
+        back = lon - step + lon_count if going_east else lon + step
+        landed(cap_ref.at[lax.rem(back, lon_count)], ring_recv.at[0 if going_east else 1, step - 1])
+
+    @pl.when(jnp.logical_not(at_pole))
+    def _():
+        landed(cap_ref.at[lon], cap_recv)
+        ring(1, True).start()
+        ring(1, False).start()
+
+    for slot in range(4):
+        landed(halo_ref.at[slot], halo_recv.at[slot])
+    corners = [
+        send(halo_ref, west_halo_ref, corner_send.at[0], corner_recv.at[0], (lat, east_lon)),
+        send(halo_ref, east_halo_ref, corner_send.at[1], corner_recv.at[1], (lat, west_lon)),
+    ]
+
+    @pl.when(jnp.logical_not(at_pole))
+    def _():
+        for step in range(2, half + 1):
+            got(step - 1, True)
+            ring(step, True).start()
+            if step < half:
+                got(step - 1, False)
+                ring(step, False).start()
+        got(half, True)
+        got(half - 1, False)
+        landed(query_ref, query_recv)
+        for step in range(1, half + 1):
+            ring(step, True).wait_send()
+            if step < half:
+                ring(step, False).wait_send()
+
+    for copy in sides:
+        copy.wait_send()
+    for copy in wide + corners:
+        copy.wait()
+
+    @pl.when(at_pole)
+    def _():
+        for src, dst, send_sem, recv_sem, to in gifts():
+            pltpu.make_async_remote_copy(
+                src_ref=src, dst_ref=dst, send_sem=send_sem, recv_sem=recv_sem,
+                device_id=at_device(*to), device_id_type=pl.DeviceIdType.MESH,
+            ).wait_send()
+
+
 def per_device(tokens, neighbor_mask, w_query, w_key, w_value, w_out):
     lat_count = lax.axis_size("lat")
     lon_count = lax.axis_size("lon")
-    lat = lax.axis_index("lat")
-    at_north = lat == 0
-    at_south = lat == lat_count - 1
     last = lat_count - 1
     params = pltpu.CompilerParams(vmem_limit_bytes=VMEM_LIMIT)
-    eastward = [(j, (j + 1) % lon_count) for j in range(lon_count)]
-    westward = [((j + 1) % lon_count, j) for j in range(lon_count)]
-
-    west = lax.ppermute(tokens, "lon", eastward)
-    east = lax.ppermute(tokens, "lon", westward)
-    north = lax.ppermute(tokens[ROWS - RADIUS :], "lat", [(i, i + 1) for i in range(last)])
-    south = lax.ppermute(tokens[:RADIUS], "lat", [(i + 1, i) for i in range(last)])
-    pole_row = jnp.where(at_north, tokens[:1], tokens[ROWS - 1 :])
     half = lon_count // 2
-    far = lax.ppermute(pole_row, "lon", [(j, (j + half) % lon_count) for j in range(lon_count)])
-    cap = jnp.where(at_north, tokens[:3], tokens[ROWS - 3 :][::-1])
-    given = []
-    for r in range(3):
-        rows = cap[:1] if r == 0 else jnp.concatenate([cap[:1], cap[r : r + 1]], axis=0)
-        given.append(lax.ppermute(rows, "lat", [(0, 1 + r), (last, last - 1 - r)]))
-    helper = jnp.minimum(lat, last - lat)
-    query_tokens = given[0][0] + given[1][0] + given[2][0]
-    key_tokens = given[0][0] + given[1][1] + given[2][1]
-    cap_tokens = lax.all_gather(key_tokens, "lon", axis=0, tiled=True)
-    halo = jnp.concatenate(
-        [
-            north[:1],
-            jnp.where(at_north, far, north[1:]),
-            jnp.where(at_south, far, south[:1]),
-            south[1:],
+    strip = lambda *dims: jax.ShapeDtypeStruct((*dims, BLOCK, WIDTH), BF16)
+    west, east, halo, west_halo, east_halo, query_tokens, cap_blocks = pl.pallas_call(
+        exchange_kernel,
+        out_shape=[strip(ROWS), strip(ROWS), strip(4), strip(4), strip(4), strip(), strip(lon_count)],
+        in_specs=[ANY_SPEC],
+        out_specs=[ANY_SPEC] * 7,
+        scratch_shapes=[
+            pltpu.SemaphoreType.DMA((2,)), pltpu.SemaphoreType.DMA((2,)),
+            pltpu.SemaphoreType.DMA((4,)), pltpu.SemaphoreType.DMA((4,)),
+            pltpu.SemaphoreType.DMA((2,)), pltpu.SemaphoreType.DMA((2,)),
+            pltpu.SemaphoreType.DMA((6,)), pltpu.SemaphoreType.DMA, pltpu.SemaphoreType.DMA,
+            pltpu.SemaphoreType.DMA((2, half)), pltpu.SemaphoreType.DMA((2, half)),
         ],
-        axis=0,
-    )
-    west_halo = lax.ppermute(halo, "lon", eastward)
-    east_halo = lax.ppermute(halo, "lon", westward)
+        compiler_params=pltpu.CompilerParams(collective_id=0, has_side_effects=True),
+        name="exchange_tokens",
+    )(tokens)
+    cap_tokens = cap_blocks.reshape(lon_count * BLOCK, WIDTH)
 
     lists = [pltpu.SMEM((272,), jnp.int32), pltpu.SMEM((272,), jnp.int32), pltpu.SMEM((2 * ROWS,), jnp.int32)]
     k_shape = lambda n: (n, BLOCK, LANES)

time: 247 us -> 247 us (level)
  the two profiles are of different devices: /device:TPU:28 before, /device:TPU:96 now
where the time goes in v2:
time: 247 us; the launch traced here: 246 us
  Pallas kernels  241 us (98%)
  starting transfers between devices  2.64 us (1%)
    pallas_call x1, Pallas kernels, per_device(): pl.pallas_call(frame_kernel, out_shape=jax.ShapeDtypeStruct((ROWS, BLOCK,...  146 us
    pallas_call x1, Pallas kernels, per_device(): pl.pallas_call(exchange_kernel, out_shape=[strip(ROWS), strip(ROWS), stri...  52.9 us
    pallas_call x1, Pallas kernels, per_device(): pl.pallas_call(cap_kernel, out_shape=jax.ShapeDtypeStruct((WIDTH + 2 * HE...  26 us
    pallas_call x1, Pallas kernels, per_device(): pl.pallas_call(own_kernel, out_shape=[jax.ShapeDtypeStruct(k_shape(ROWS),...  15 us
  transfers between devices with their start and end apart: 3, of which 0 were waited for; matrix products, arithmetic and copies ran while one was open for 0% of the time, Pallas kernels for 65%

profile of v2, /device:TPU:96, one launch (start us, length us, event | category | flops | bytes accessed | tf_op | source)
XLA Modules:
  0.0 246.2 jit_solution(7343952291792886602)
XLA Ops:
  0.0 52.9 %exchange_tokens.1 = (bf16[12,128,384]{2,1,0:T(8,128)(2,1)}, bf16[12,128,384]{2,1,0:T(8,128)(2,1)}, bf16[4,128,384]{2,1,0:T(8,128)(2,1)}, bf16[4,128,384]{2,1,0:...) custom-call(bf16[12,128,384]{2,1,0:T(8,128)(2,1)} %tokens_ref.3), custom_call_target="tpu_custom_call" | custom-call | tf_op jit(solution)/shard_map/exchange_tokens/pallas_call | solution.py:550
  52.9 0.0 copy-start.3
  52.9 26.0 %cap_rows.1 = f32[400,128]{1,0:T(8,128)} custom-call(bf16[128,384]{1,0:T(8,128)(2,1)} %get-tuple-element.18.query_tokens_ref, bf16[2048,384]{1,0:T(8,128)(2,1)} %bitcast.1, bf16[384,384]{1,0:T(8,128)(2,1)} %w_query_ref.3, bf16[384,384]{1,0:T(8,128)(2,1)} %w_key_ref.5, bf16[384,384]{1,0:T(8,128)(2,1)} %w_value_ref.5), custom_call_target="tpu_custom_call" | custom-call | flops 4000000000 | bytes 3145728 | tf_op jit(solution)/shard_map/cap_rows/pallas_call | solution.py:598
  78.9 0.7 collective-permute-start.2
  79.6 0.7 collective-permute-start.1
  80.2 1.3 collective-permute-start
  81.5 0.0 copy-done.3
  81.6 0.7 copy.10.mask_ref
  82.3 15.0 %own_column.1 = (bf16[12,128,512]{2,1,0:T(8,128)(2,1)}, bf16[12,4,112,128]{3,2,1,0:T(8,128)(2,1)}, bf16[12,4,128,256]{3,2,1,0:T(8,128)(2,1)}, f32[12,4,48,128]{3...) custom-call(s32[12,5,3]{2,1,0:T(8,128)} %copy.10.mask_ref, bf16[12,128,384]{2,1,0:T(8,128)(2,1)} %tokens_ref.3, ...), custom_call_target="tpu_custom_call" | custom-call | flops 8000000000 | bytes 12582912 | tf_op jit(solution)/shard_map/own_column/pallas_call | solution.py:574
  97.4 145.8 %frame_columns.1.layer_ref = bf16[12,128,384]{2,1,0:T(8,128)(2,1)} custom-call(s32[12,5,3]{2,1,0:T(8,128)} %copy.10.mask_ref, bf16[12,128,384]{2,1,0:T(8,128)(2,1)} %get-tuple-element.20.west_ref, bf16[12,128,384]{2,1,0:T(8,128)(2,1)} %get-tuple-element.21.east_ref, bf16[4,128,384]{2,1,0:T(8,128)(2,1)} %get-tuple-element.22.halo_ref, ...), custom_call_target="tpu_custom_call" | custom-call | flops 12000000000 | bytes 16777216 | tf_op jit(solution)/shard_map/frame_columns/pallas_call | solution.py:619
  243.1 0.0 collective-permute-done.2.c_ref
  243.1 0.0 copy-start
  243.1 0.0 collective-permute-done.1.b_ref
  243.2 0.0 copy-start.1
  243.2 0.0 collective-permute-done.a_ref
  243.2 0.6 copy-done
  243.8 0.1 copy-done.1
  243.9 0.0 copy-start.2
  243.9 0.7 copy-done.2
  244.6 1.6 join_cap.1
Async XLA Ops:
  52.9 28.7 %copy-start.3 = (s32[12,5,3]{0,2,1:T(4,128)S(1)}, s32[12,5,3]{0,2,1:T(4,128)}, u32[]{:S(2)}) copy-start(s32[12,5,3]{0,2,1:T(4,128)} %param.7) | copy-start | bytes 2164
  78.9 164.2 %collective-permute-start.2 = (f32[400,128]{1,0:T(8,128)}, f32[400,128]{1,0:T(8,128)S(1)}, u32[]{:S(2)}, u32[]{:S(2)}) collective-permute-start(f32[400,128]{1,0:T(8,128)} %cap_rows.1), channel_id=1, source_target_pairs={{48,0},{64,112},{49,1},{65,113},{50,2},{66,114},{51,3},{67,115},{5... | collective-permute-start | bytes 614408 | tf_op jit(solution)/shard_map/ppermute | solution.py:617
  79.6 163.6 %collective-permute-start.1 = (f32[400,128]{1,0:T(8,128)}, f32[400,128]{1,0:T(8,128)S(1)}, u32[]{:S(2)}, u32[]{:S(2)}) collective-permute-start(f32[400,128]{1,0:T(8,128)} %cap_rows.1), channel_id=1, source_target_pairs={{32,0},{80,112},{33,1},{81,113},{34,2},{82,114},{35,3},{83,115},{3... | collective-permute-start | bytes 614408 | tf_op jit(solution)/shard_map/ppermute | solution.py:617
  80.2 162.9 %collective-permute-start = (f32[400,128]{1,0:T(8,128)}, f32[400,128]{1,0:T(8,128)S(1)}, u32[]{:S(2)}, u32[]{:S(2)}) collective-permute-start(f32[400,128]{1,0:T(8,128)} %cap_rows.1), channel_id=1, source_target_pairs={{16,0},{96,112},{17,1},{97,113},{18,2},{98,114},{19,3},{99,115},{2... | collective-permute-start | bytes 614408 | tf_op jit(solution)/shard_map/ppermute | solution.py:617
  243.1 0.7 copy-start
  243.2 0.7 copy-start.1
  243.9 0.7 copy-start.2

commit v3 on v1

--- a/solution.py
+++ b/solution.py
@@ -397,44 +397,252 @@
         copy.wait()
 
 
+def at_device(lat, lon):
+    return {"lat": lat, "lon": lon}
+
+
+def remote(src, dst, send_sem, recv_sem, to):
+    return pltpu.make_async_remote_copy(
+        src_ref=src, dst_ref=dst, send_sem=send_sem, recv_sem=recv_sem,
+        device_id=at_device(*to), device_id_type=pl.DeviceIdType.MESH,
+    )
+
+
+def landed(dst, sem):
+    pltpu.make_async_copy(dst, dst, sem).wait()
+
+
+class Plan:
+    def __init__(self):
+        self.lat, self.lon = lat, lon = lax.axis_index("lat"), lax.axis_index("lon")
+        self.lon_count, self.last = lax.axis_size("lon"), lax.axis_size("lat") - 1
+        self.half = half = self.lon_count // 2
+        self.is_north, self.is_south = lat == 0, lat == self.last
+        self.at_pole = jnp.logical_or(self.is_north, self.is_south)
+        self.east = (lat, lax.rem(lon + 1, self.lon_count))
+        self.west = (lat, lax.rem(lon + self.lon_count - 1, self.lon_count))
+        self.far = (lat, lax.rem(lon + half, self.lon_count))
+        self.odd = lax.rem(lon, 2) == 1
+        self.place = lax.rem(lon, half)
+        self.side = lon // half
+        base = lon - self.place
+        self.ring_east = (lat, base + lax.rem(self.place + 1, half))
+        self.ring_west = (lat, base + lax.rem(self.place + half - 1, half))
+        flip = lat + 1 - 2 * lax.rem(lat, 2)
+        first_half = self.side == 0
+        self.relay = (jnp.where(first_half, flip, lat), self.far[1])
+        self.source = (jnp.where(first_half, lat, flip), self.far[1])
+        self.pole = jnp.where(lat < (self.last + 1) // 2, 0, self.last)
+
+    def relay_of(self, lat):
+        flip = lat + 1 - 2 * lax.rem(lat, 2)
+        return (jnp.where(self.side == 0, flip, lat), self.far[1])
+
+    def helper(self, r):
+        return (jnp.where(self.is_north, 1 + r, self.last - 1 - r), self.lon)
+
+    def cap_row(self, r):
+        return jnp.where(self.is_north, r, ROWS - 1 - r)
+
+
+def meet(plan):
+    barrier = pltpu.get_barrier_semaphore()
+
+    def tell(to):
+        pl.semaphore_signal(barrier, inc=1, device_id=at_device(*to), device_id_type=pl.DeviceIdType.MESH)
+
+    def tell_if(wanted, to):
+        @pl.when(wanted)
+        def _():
+            tell(to)
+
+    even = jnp.logical_not(plan.odd)
+    inner = jnp.logical_not(plan.at_pole)
+    lat, lon, last = plan.lat, plan.lon, plan.last
+    tell(plan.east)
+    tell(plan.west)
+    tell_if(jnp.logical_and(even, lat < last), (lat + 1, lon))
+    tell_if(jnp.logical_and(even, lat > 0), (lat - 1, lon))
+    tell_if(plan.odd, plan.source)
+    tell_if(jnp.logical_and(plan.odd, lat < last), plan.relay_of(lat + 1))
+    tell_if(jnp.logical_and(plan.odd, lat > 0), plan.relay_of(lat - 1))
+    tell_if(plan.at_pole, plan.far)
+    tell_if(inner, (plan.pole, lon))
+    tell_if(inner, plan.far)
+    tell_if(inner, plan.ring_east)
+    tell_if(inner, plan.ring_west)
+    to_lat = jnp.where(plan.odd, plan.source[0], lat)
+    count = 2 + jnp.where(to_lat < last, 1, 0) + jnp.where(to_lat > 0, 1, 0)
+    count = count + jnp.where(plan.odd, 1, 0) + jnp.where(plan.at_pole, 4, 3)
+    pl.semaphore_wait(barrier, count)
+
+
+def exchange_kernel(
+    tokens_ref, west_ref, east_ref, halo_ref, west_halo_ref, east_halo_ref, query_ref, cap_ref, relay_ref,
+    side_send, side_recv, halo_send, halo_recv, far_send, far_recv, relay_send, relay_recv, corner_send, corner_recv,
+    give_send, query_recv, cap_recv, sib_send, sib_recv, ring_send, ring_recv,
+):
+    plan = Plan()
+    lat, lon, last = plan.lat, plan.lon, plan.last
+    inner = jnp.logical_not(plan.at_pole)
+    even = jnp.logical_not(plan.odd)
+    ends = (pl.ds(ROWS - RADIUS, RADIUS), pl.ds(0, RADIUS))
+    pairs = (pl.ds(0, RADIUS), pl.ds(RADIUS, RADIUS))
+    meet(plan)
+
+    def gifts():
+        copies = []
+        for r in range(3):
+            row, first = plan.cap_row(r), plan.cap_row(0)
+            to = plan.helper(r)
+            copies.append(remote(
+                tokens_ref.at[row], cap_ref.at[plan.place, plan.side], give_send.at[r], cap_recv, to))
+            copies.append(remote(tokens_ref.at[first], query_ref, give_send.at[3 + r], query_recv, to))
+        return copies
+
+    def far_rows():
+        copies = []
+        for n in range(RADIUS):
+            row = jnp.where(plan.is_north, n, ROWS - 1 - n)
+            slot = jnp.where(plan.is_north, RADIUS - 1 - n, RADIUS + n)
+            copies.append(remote(
+                tokens_ref.at[row], halo_ref.at[slot], far_send.at[n], far_recv.at[n], plan.far))
+        return copies
+
+    def lat_rows(n):
+        to = (lat + 1 - 2 * n, lon)
+        return remote(tokens_ref.at[ends[n]], halo_ref.at[pairs[n]], halo_send.at[n], halo_recv.at[n], to)
+
+    def lat_rows_by_relay(n):
+        return remote(tokens_ref.at[ends[n]], relay_ref.at[pairs[n]], halo_send.at[n], relay_recv.at[n], plan.relay)
+
+    def relayed(n):
+        to = (plan.source[0] + 1 - 2 * n, plan.source[1])
+        return remote(relay_ref.at[pairs[n]], halo_ref.at[pairs[n]], relay_send.at[n], halo_recv.at[n], to)
+
+    def has(n, at):
+        return at < last if n == 0 else at > 0
+
+    def when_each(wanted, act):
+        for n in range(2):
+            @pl.when(wanted(n))
+            def _(n=n):
+                act(n)
+
+    @pl.when(plan.at_pole)
+    def _():
+        for copy in gifts() + far_rows():
+            copy.start()
+
+    when_each(lambda n: jnp.logical_and(even, has(n, lat)), lambda n: lat_rows(n).start())
+    when_each(lambda n: jnp.logical_and(plan.odd, has(n, lat)), lambda n: lat_rows_by_relay(n).start())
+    wide = [
+        remote(tokens_ref, west_ref, side_send.at[0], side_recv.at[0], plan.east),
+        remote(tokens_ref, east_ref, side_send.at[1], side_recv.at[1], plan.west),
+    ]
+    for copy in wide:
+        copy.start()
+
+    def pass_on(n):
+        landed(relay_ref.at[pairs[n]], relay_recv.at[n])
+        relayed(n).start()
+
+    when_each(lambda n: jnp.logical_and(plan.odd, has(n, plan.source[0])), pass_on)
+
+    mine = cap_ref.at[plan.place, plan.side]
+    theirs = cap_ref.at[plan.place, 1 - plan.side]
+    sibling = remote(mine, mine, sib_send, sib_recv, plan.far)
+
+    @pl.when(inner)
+    def _():
+        landed(mine, cap_recv)
+        sibling.start()
+
+    count = plan.half
+    east_steps, west_steps = count // 2, count // 2 - 1
+
+    def ring(step, eastward):
+        shift = count - (step - 1) if eastward else step - 1
+        spot = cap_ref.at[lax.rem(plan.place + shift, count)]
+        n = 0 if eastward else 1
+        return remote(
+            spot, spot, ring_send.at[n, step - 1], ring_recv.at[n, step - 1],
+            plan.ring_east if eastward else plan.ring_west)
+
+    def got(step, eastward):
+        shift = count - step if eastward else step
+        spot = cap_ref.at[lax.rem(plan.place + shift, count)]
+        landed(spot, ring_recv.at[0 if eastward else 1, step - 1])
+
+    @pl.when(inner)
+    def _():
+        landed(theirs, sib_recv)
+        ring(1, True).start()
+        ring(1, False).start()
+
+    when_each(lambda n: has(1 - n, lat), lambda n: landed(halo_ref.at[pairs[n]], halo_recv.at[n]))
+
+    @pl.when(plan.at_pole)
+    def _():
+        for n in range(RADIUS):
+            landed(halo_ref.at[jnp.where(plan.is_north, RADIUS - 1 - n, RADIUS + n)], far_recv.at[n])
+
+    corners = [
+        remote(halo_ref, west_halo_ref, corner_send.at[0], corner_recv.at[0], plan.east),
+        remote(halo_ref, east_halo_ref, corner_send.at[1], corner_recv.at[1], plan.west),
+    ]
+    for copy in corners:
+        copy.start()
+
+    @pl.when(inner)
+    def _():
+        for step in range(2, east_steps + 1):
+            got(step - 1, True)
+            ring(step, True).start()
+            if step <= west_steps:
+                got(step - 1, False)
+                ring(step, False).start()
+        got(east_steps, True)
+        got(west_steps, False)
+        landed(query_ref, query_recv)
+        sibling.wait_send()
+        for step in range(1, east_steps + 1):
+            ring(step, True).wait_send()
+            if step <= west_steps:
+                ring(step, False).wait_send()
+
+    for copy in wide + corners:
+        copy.wait()
+    when_each(lambda n: jnp.logical_and(even, has(n, lat)), lambda n: lat_rows(n).wait_send())
+    when_each(lambda n: jnp.logical_and(plan.odd, has(n, lat)), lambda n: lat_rows_by_relay(n).wait_send())
+    when_each(lambda n: jnp.logical_and(plan.odd, has(n, plan.source[0])), lambda n: relayed(n).wait_send())
+
+    @pl.when(plan.at_pole)
+    def _():
+        for copy in gifts() + far_rows():
+            copy.wait_send()
+
+
 def per_device(tokens, neighbor_mask, w_query, w_key, w_value, w_out):
     lat_count = lax.axis_size("lat")
     lon_count = lax.axis_size("lon")
-    lat = lax.axis_index("lat")
-    at_north = lat == 0
-    at_south = lat == lat_count - 1
     last = lat_count - 1
     params = pltpu.CompilerParams(vmem_limit_bytes=VMEM_LIMIT)
-    eastward = [(j, (j + 1) % lon_count) for j in range(lon_count)]
-    westward = [((j + 1) % lon_count, j) for j in range(lon_count)]
-
-    west = lax.ppermute(tokens, "lon", eastward)
-    east = lax.ppermute(tokens, "lon", westward)
-    north = lax.ppermute(tokens[ROWS - RADIUS :], "lat", [(i, i + 1) for i in range(last)])
-    south = lax.ppermute(tokens[:RADIUS], "lat", [(i + 1, i) for i in range(last)])
-    pole_row = jnp.where(at_north, tokens[:1], tokens[ROWS - 1 :])
     half = lon_count // 2
-    far = lax.ppermute(pole_row, "lon", [(j, (j + half) % lon_count) for j in range(lon_count)])
-    cap = jnp.where(at_north, tokens[:3], tokens[ROWS - 3 :][::-1])
-    given = []
-    for r in range(3):
-        rows = cap[:1] if r == 0 else jnp.concatenate([cap[:1], cap[r : r + 1]], axis=0)
-        given.append(lax.ppermute(rows, "lat", [(0, 1 + r), (last, last - 1 - r)]))
-    helper = jnp.minimum(lat, last - lat)
-    query_tokens = given[0][0] + given[1][0] + given[2][0]
-    key_tokens = given[0][0] + given[1][1] + given[2][1]
-    cap_tokens = lax.all_gather(key_tokens, "lon", axis=0, tiled=True)
-    halo = jnp.concatenate(
-        [
-            north[:1],
-            jnp.where(at_north, far, north[1:]),
-            jnp.where(at_south, far, south[:1]),
-            south[1:],
+    strip = lambda *dims: jax.ShapeDtypeStruct((*dims, BLOCK, WIDTH), BF16)
+    dma = pltpu.SemaphoreType.DMA
+    west, east, halo, west_halo, east_halo, query_tokens, cap_blocks, _ = pl.pallas_call(
+        exchange_kernel,
+        out_shape=[
+            strip(ROWS), strip(ROWS), strip(4), strip(4), strip(4), strip(), strip(half, 2), strip(4),
         ],
-        axis=0,
-    )
-    west_halo = lax.ppermute(halo, "lon", eastward)
-    east_halo = lax.ppermute(halo, "lon", westward)
+        in_specs=[ANY_SPEC],
+        out_specs=[ANY_SPEC] * 8,
+        scratch_shapes=[dma((2,))] * 10 + [dma((6,)), dma, dma, dma, dma, dma((2, half // 2)), dma((2, half // 2))],
+        compiler_params=pltpu.CompilerParams(collective_id=0, has_side_effects=True),
+        name="exchange_tokens",
+    )(tokens)
+    cap_tokens = cap_blocks.reshape(lon_count * BLOCK, WIDTH)
 
     lists = [pltpu.SMEM((272,), jnp.int32), pltpu.SMEM((272,), jnp.int32), pltpu.SMEM((2 * ROWS,), jnp.int32)]
     k_shape = lambda n: (n, BLOCK, LANES)

time: 247 us -> 239 us (0.968)
  the two profiles are of different devices: /device:TPU:28 before, /device:TPU:0 now
where the time goes in v3:
time: 239 us; the launch traced here: 237 us
  Pallas kernels  231 us (97%)
  starting transfers between devices  3.86 us (2%)
    pallas_call x1, Pallas kernels, per_device(): pl.pallas_call(frame_kernel, out_shape=jax.ShapeDtypeStruct((ROWS, BLOCK,...  166 us
    pallas_call x1, Pallas kernels, per_device(): pl.pallas_call(exchange_kernel, out_shape=[strip(ROWS), strip(ROWS), stri...  46.6 us
    pallas_call x1, Pallas kernels, per_device(): pl.pallas_call(own_kernel, out_shape=[jax.ShapeDtypeStruct(k_shape(ROWS),...  13.2 us
  transfers between devices with their start and end apart: 3, of which 0 were waited for; matrix products, arithmetic and copies ran while one was open for 0% of the time, Pallas kernels for 76%

profile of v3, /device:TPU:0, one launch (start us, length us, event | category | flops | bytes accessed | tf_op | source)
XLA Modules:
  0.0 237.2 jit_solution(17019817485510348000)
XLA Ops:
  0.0 46.6 %exchange_tokens.1 = (bf16[12,128,384]{2,1,0:T(8,128)(2,1)}, bf16[12,128,384]{2,1,0:T(8,128)(2,1)}, bf16[4,128,384]{2,1,0:T(8,128)(2,1)}, bf16[4,128,384]{2,1,0:...) custom-call(bf16[12,128,384]{2,1,0:T(8,128)(2,1)} %tokens_ref.3), custom_call_target="tpu_custom_call" | custom-call | tf_op jit(solution)/shard_map/exchange_tokens/pallas_call | solution.py:634
  46.6 0.0 copy-start.3
  46.6 2.3 cap_rows.1
  49.0 1.3 collective-permute-start.2
  50.3 1.3 collective-permute-start.1
  51.6 1.3 collective-permute-start
  52.9 0.0 copy-done.3
  52.9 0.7 copy.10.mask_ref
  53.6 13.2 %own_column.1 = (bf16[12,128,512]{2,1,0:T(8,128)(2,1)}, bf16[12,4,112,128]{3,2,1,0:T(8,128)(2,1)}, bf16[12,4,128,256]{3,2,1,0:T(8,128)(2,1)}, f32[12,4,48,128]{3...) custom-call(s32[12,5,3]{2,1,0:T(8,128)} %copy.10.mask_ref, bf16[12,128,384]{2,1,0:T(8,128)(2,1)} %tokens_ref.3, ...), custom_call_target="tpu_custom_call" | custom-call | flops 8000000000 | bytes 12582912 | tf_op jit(solution)/shard_map/own_column/pallas_call | solution.py:654
  66.8 166.4 %frame_columns.1.layer_ref = bf16[12,128,384]{2,1,0:T(8,128)(2,1)} custom-call(s32[12,5,3]{2,1,0:T(8,128)} %copy.10.mask_ref, bf16[12,128,384]{2,1,0:T(8,128)(2,1)} %get-tuple-element.20.west_ref, bf16[12,128,384]{2,1,0:T(8,128)(2,1)} %get-tuple-element.21.east_ref, bf16[4,128,384]{2,1,0:T(8,128)(2,1)} %get-tuple-element.22.halo_ref, ...), custom_call_target="tpu_custom_call" | custom-call | flops 12000000000 | bytes 16777216 | tf_op jit(solution)/shard_map/frame_columns/pallas_call | solution.py:699
  233.2 0.0 collective-permute-done.2.c_ref
  233.2 0.0 copy-start
  233.2 0.0 collective-permute-done.1.b_ref
  233.2 0.0 copy-start.1
  233.3 0.0 collective-permute-done.a_ref
  233.3 0.6 copy-done
  233.9 0.1 copy-done.1
  234.0 0.0 copy-start.2
  234.0 0.7 copy-done.2
  234.7 2.6 %join_cap.1 = bf16[12,128,384]{2,1,0:T(8,128)(2,1)} custom-call(s32[12,5,3]{2,1,0:T(8,128)} %copy.10.mask_ref, f32[400,128]{1,0:T(8,128)} %copy-done.2, f32[400,128]{1,0:T(8,128)} %copy-done.1, f32[400,128]{1,0:T(8,128)} %copy-done, bf16[384,384]{1,0:T(8,128)(2,1)} %w_out_ref.3, ...), custom_call_target="tpu_custom_call", output_to_operand_aliasing={{}: (5, {})} | custom-call | tf_op jit(solution)/shard_map/join_cap/pallas_call | solution.py:718
Async XLA Ops:
  46.6 6.2 %copy-start.3 = (s32[12,5,3]{0,2,1:T(4,128)S(1)}, s32[12,5,3]{0,2,1:T(4,128)}, u32[]{:S(2)}) copy-start(s32[12,5,3]{0,2,1:T(4,128)} %param.7) | copy-start | bytes 2164
  49.0 184.2 %collective-permute-start.2 = (f32[400,128]{1,0:T(8,128)}, f32[400,128]{1,0:T(8,128)S(1)}, u32[]{:S(2)}, u32[]{:S(2)}) collective-permute-start(f32[400,128]{1,0:T(8,128)} %cap_rows.1), channel_id=1, source_target_pairs={{48,0},{64,112},{49,1},{65,113},{50,2},{66,114},{51,3},{67,115},{5... | collective-permute-start | bytes 614408 | tf_op jit(solution)/shard_map/ppermute | solution.py:697
  50.3 183.0 %collective-permute-start.1 = (f32[400,128]{1,0:T(8,128)}, f32[400,128]{1,0:T(8,128)S(1)}, u32[]{:S(2)}, u32[]{:S(2)}) collective-permute-start(f32[400,128]{1,0:T(8,128)} %cap_rows.1), channel_id=1, source_target_pairs={{32,0},{80,112},{33,1},{81,113},{34,2},{82,114},{35,3},{83,115},{3... | collective-permute-start | bytes 614408 | tf_op jit(solution)/shard_map/ppermute | solution.py:697
  51.6 181.7 %collective-permute-start = (f32[400,128]{1,0:T(8,128)}, f32[400,128]{1,0:T(8,128)S(1)}, u32[]{:S(2)}, u32[]{:S(2)}) collective-permute-start(f32[400,128]{1,0:T(8,128)} %cap_rows.1), channel_id=1, source_target_pairs={{16,0},{96,112},{17,1},{97,113},{18,2},{98,114},{19,3},{99,115},{2... | collective-permute-start | bytes 614408 | tf_op jit(solution)/shard_map/ppermute | solution.py:697
  233.2 0.7 copy-start
  233.2 0.7 copy-start.1
  234.0 0.7 copy-start.2

commit v4 on v0

v4 whole, which is shorter than its diff:
```python
import functools

import jax
import jax.numpy as jnp
from jax import lax
from jax.experimental import pallas as pl
from jax.experimental.pallas import tpu as pltpu
from jax.sharding import PartitionSpec as P

HEADS = 8
HEAD_DIM = 48
PAIRS = 4
WIDTH = 384
BLOCK = 128
ROWS = 12
RADIUS = 2
SPAN = 5
FRAME = ROWS + 2 * RADIUS
SLOTS = 3 * FRAME
VROWS = 112
LANES = 128 * PAIRS
AHEAD = 8
CHUNKS = 3
SCORE_SCALE = HEAD_DIM ** -0.5 * 1.4426950408889634
SUM_LOW = 1e-30
SUM_HIGH = 1e30
VMEM_LIMIT = 56 * 2**20
F32 = jnp.float32
BF16 = jnp.bfloat16
VMEM_SPEC = pl.BlockSpec(memory_space=pltpu.VMEM)
SMEM_SPEC = pl.BlockSpec(memory_space=pltpu.SMEM)
ANY_SPEC = pl.BlockSpec(memory_space=pl.ANY)


def dot(a, b, dims=((1,), (0,))):
    return lax.dot_general(a, b, (dims, ((), ())), preferred_element_type=F32)


def prepare_keys(w_key_ref, wide_ref):
    wide_ref[...] = jnp.zeros_like(wide_ref)
    for p in range(PAIRS):
        wide_ref[:, 128 * p : 128 * p + 96] = w_key_ref[:, 96 * p : 96 * p + 96]


def flipped(ref):
    return ref[...].astype(F32).T.astype(BF16)


def put_keys_values(tokens, slots, wide_ref, value_t_ref, k_ref, vt_ref):
    keys = dot(tokens, wide_ref[...]).astype(BF16)
    values = dot(value_t_ref[...], tokens, ((1,), (1,))).astype(BF16)
    for n, slot in enumerate(slots):
        k_ref[slot] = keys[128 * n : 128 * n + 128]
        for p in range(PAIRS):
            vt_ref[slot, p, 0:96] = values[96 * p : 96 * p + 96, 128 * n : 128 * n + 128]


def put_queries(tokens, rows, query_t_ref, qd_ref):
    queries = dot(query_t_ref[...], tokens, ((1,), (1,))).astype(BF16)
    for n, row in enumerate(rows):
        for p in range(PAIRS):
            part = queries[96 * p : 96 * p + 96, 128 * n : 128 * n + 128]
            qd_ref[row, p, 0:48, 0:128] = part[0:48]
            qd_ref[row, p, 48:96, 128:256] = part[48:96]


def put_ones(vt_ref):
    ones = jnp.ones((VROWS - 96, 128), BF16)

    def body(slot, carry):
        for p in range(PAIRS):
            vt_ref[slot, p, 96:VROWS] = ones
        return carry

    lax.fori_loop(0, vt_ref.shape[0], body, 0)


def safe_row(q, acc_at, begin, end, slot_of, k_ref, vt_ref, qd_ref, acc_ref, top_ref):
    top_ref[...] = jnp.full(top_ref.shape, -jnp.inf, F32)

    def scores(n, p):
        return dot(k_ref[slot_of(n), :, 128 * p : 128 * p + 128], qd_ref[q, p]) * SCORE_SCALE

    def find_top(n, carry):
        for p in range(PAIRS):
            top_ref[p] = jnp.maximum(top_ref[p], jnp.max(scores(n, p), axis=0, keepdims=True))
        return carry

    lax.fori_loop(begin, end, find_top, 0)
    acc_ref[acc_at] = jnp.zeros(acc_ref.shape[1:], F32)

    def add(n, carry):
        for p in range(PAIRS):
            weights = jnp.exp2(scores(n, p) - top_ref[p, 0:1]).astype(BF16)
            acc_ref[acc_at, p] += dot(vt_ref[slot_of(n), p], weights)
        return carry

    lax.fori_loop(begin, end, add, 0)


def sums_hold(sums):
    return jnp.where((sums >= SUM_LOW) & (sums <= SUM_HIGH), 1.0, 0.0)


def normalised(acc_ref, row):
    parts = []
    for p in range(PAIRS):
        sums = 1.0 / acc_ref[row, p, 96:97, :]
        parts.append(acc_ref[row, p, 0:48, 0:128] * sums[:, 0:128])
        parts.append(acc_ref[row, p, 48:96, 128:256] * sums[:, 128:256])
    return jnp.concatenate(parts, axis=0).astype(BF16)


def masked_values(vt_ref, slot, p, bit):
    return vt_ref[slot, p] * jnp.full((VROWS, BLOCK), bit, F32).astype(BF16)


def attend(rows, columns, mask_ref, k_ref, vt_ref, qd_ref, acc_ref):
    tiles = []
    for i in rows:
        blocks = [
            (e * FRAME + i + d, mask_ref[i, d, e].astype(F32)) for e in columns for d in range(SPAN)
        ]
        tiles += [(i, blocks[n : n + 2]) for n in range(0, len(blocks), 2)]
    chunks = [(i, tile, p) for i, tile in tiles for p in range(PAIRS)]

    def scores(chunk):
        i, tile, p = chunk
        keys = [k_ref[slot, :, 128 * p : 128 * p + 128] for slot, _ in tile]
        return dot(jnp.concatenate(keys, axis=0) if len(keys) > 1 else keys[0], qd_ref[i, p])

    def values(chunk, weights):
        i, tile, p = chunk
        parts = [masked_values(vt_ref, slot, p, bit) for slot, bit in tile]
        return dot(jnp.concatenate(parts, axis=1) if len(parts) > 1 else parts[0], weights)

    held = {}
    for step in range(len(chunks) + AHEAD):
        if step < len(chunks):
            held[step] = scores(chunks[step])
        if step >= AHEAD:
            chunk = chunks[step - AHEAD]
            weights = jnp.exp2(held.pop(step - AHEAD) * SCORE_SCALE).astype(BF16)
            acc_ref[chunk[0], chunk[2]] += values(chunk, weights)


def attend_cap(blocks, k_ref, vt_ref, qd_ref, acc_ref, top_ref):
    def scores(p):
        qd = qd_ref[0, p]
        return [
            dot(jnp.concatenate([k_ref[n + m, :, 128 * p : 128 * p + 128] for m in range(2)], axis=0), qd)
            for n in range(0, blocks, 2)
        ]

    def finish(p, tiles):
        tops = [jnp.max(tile, axis=0, keepdims=True) for tile in tiles]
        top = functools.reduce(jnp.maximum, tops) * SCORE_SCALE
        total = None
        for n, tile in enumerate(tiles):
            weights = jnp.exp2(tile * SCORE_SCALE - top).astype(BF16)
            part = dot(jnp.concatenate([vt_ref[2 * n, p], vt_ref[2 * n + 1, p]], axis=1), weights)
            total = part if total is None else total + part
        acc_ref[p] = total
        top_ref[p, 0:1] = top

    held = scores(0)
    for p in range(PAIRS):
        later = scores(p + 1) if p + 1 < PAIRS else None
        finish(p, held)
        held = later


def at_device(lat, lon):
    return {"lat": lat, "lon": lon}


def remote(src, dst, send_sem, recv_sem, to):
    return pltpu.make_async_remote_copy(
        src_ref=src, dst_ref=dst, send_sem=send_sem, recv_sem=recv_sem,
        device_id=at_device(*to), device_id_type=pl.DeviceIdType.MESH,
    )


def landed(dst, sem):
    pltpu.make_async_copy(dst, dst, sem).wait()


class Plan:
    def __init__(self):
        self.lat, self.lon = lat, lon = lax.axis_index("lat"), lax.axis_index("lon")
        self.lon_count, self.last = lax.axis_size("lon"), lax.axis_size("lat") - 1
        self.half = half = self.lon_count // 2
        self.is_north, self.is_south = lat == 0, lat == self.last
        self.at_pole = jnp.logical_or(self.is_north, self.is_south)
        self.inner = jnp.logical_not(self.at_pole)
        self.east = (lat, lax.rem(lon + 1, self.lon_count))
        self.west = (lat, lax.rem(lon + self.lon_count - 1, self.lon_count))
        self.far = (lat, lax.rem(lon + half, self.lon_count))
        self.place = lax.rem(lon, half)
        self.side = lon // half
        base = lon - self.place
        self.ring_east = (lat, base + lax.rem(self.place + 1, half))
        self.ring_west = (lat, base + lax.rem(self.place + half - 1, half))
        north_half = lat < (self.last + 1) // 2
        self.pole = (jnp.where(north_half, 0, self.last), lon)
        self.part = jnp.where(north_half, lat - 1, self.last - 1 - lat)

    def helper(self, r):
        return (jnp.where(self.is_north, 1 + r, self.last - 1 - r), self.lon)

    def cap_row(self, r):
        return jnp.where(self.is_north, r, ROWS - 1 - r)


def tell_senders(plan):
    barrier = pltpu.get_barrier_semaphore()

    def tell(to):
        pl.semaphore_signal(barrier, inc=1, device_id=at_device(*to), device_id_type=pl.DeviceIdType.MESH)

    def tell_if(wanted, targets):
        @pl.when(wanted)
        def _():
            for to in targets:
                tell(to)

    lat, lon = plan.lat, plan.lon
    tell(plan.east)
    tell(plan.west)
    tell_if(lat < plan.last, [(lat + 1, lon)])
    tell_if(lat > 0, [(lat - 1, lon)])
    tell_if(plan.at_pole, [plan.far] + [plan.helper(r) for r in range(3)])
    tell_if(plan.inner, [plan.pole, plan.far, plan.ring_east, plan.ring_west])


def wait_receivers(plan):
    pl.semaphore_wait(pltpu.get_barrier_semaphore(), jnp.where(plan.at_pole, 7, 8))


def grid_kernel(
    mask_ref, tokens_ref, w_query_ref, w_key_ref, w_value_ref,
    mixed_ref, hold_ref, west_out, east_out, halos_out,
    west_ref, east_ref, halos_ref, query_ref, cap_ref, part_ref, back_ref,
    k_ref, vt_ref, qd_ref, acc_ref, cap_k, cap_vt, cap_qd, cap_acc, cap_top, wide_ref, query_t_ref, value_t_ref,
    side_send, side_recv, halo_send, halo_recv, far_send, far_recv, corner_send, corner_recv,
    give_send, query_recv, cap_recv, sib_send, sib_recv, ring_send, ring_recv, part_send, part_recv, keep_sem,
):
    plan = Plan()
    lat, last = plan.lat, plan.last
    ends = (pl.ds(ROWS - RADIUS, RADIUS), pl.ds(0, RADIUS))
    pairs = (pl.ds(0, RADIUS), pl.ds(RADIUS, RADIUS))
    halo_ref, west_halo_ref, east_halo_ref = halos_ref.at[0], halos_ref.at[1], halos_ref.at[2]
    chunk = ROWS // CHUNKS
    count = plan.half
    east_steps, west_steps = count // 2, count // 2 - 1

    tell_senders(plan)
    prepare_keys(w_key_ref, wide_ref)
    query_t_ref[...] = flipped(w_query_ref)
    value_t_ref[...] = flipped(w_value_ref)
    put_ones(vt_ref)
    put_ones(cap_vt)
    qd_ref[...] = jnp.zeros_like(qd_ref)
    cap_qd[...] = jnp.zeros_like(cap_qd)
    acc_ref[...] = jnp.zeros_like(acc_ref)
    hold_ref[...] = jnp.ones_like(hold_ref)
    wait_receivers(plan)

    def gifts():
        copies = []
        for r in range(3):
            to = plan.helper(r)
            copies.append(remote(
                tokens_ref.at[plan.cap_row(r)], cap_ref.at[plan.place, plan.side], give_send.at[r], cap_recv, to))
            copies.append(remote(tokens_ref.at[plan.cap_row(0)], query_ref, give_send.at[3 + r], query_recv, to))
        return copies

    def far_slot(n):
        return jnp.where(plan.is_north, RADIUS - 1 - n, RADIUS + n)

    def far_rows():
        rows = [jnp.where(plan.is_north, n, ROWS - 1 - n) for n in range(RADIUS)]
        return [
            remote(tokens_ref.at[rows[n]], halo_ref.at[far_slot(n)], far_send.at[n], far_recv.at[n], plan.far)
            for n in range(RADIUS)
        ]

    def lat_rows(n):
        to = (lat + 1 - 2 * n, plan.lon)
        return remote(tokens_ref.at[ends[n]], halo_ref.at[pairs[n]], halo_send.at[n], halo_recv.at[n], to)

    def has(n):
        return lat < last if n == 0 else lat > 0

    def when_each(wanted, act):
        for n in range(2):
            @pl.when(wanted(n))
            def _(n=n):
                act(n)

    def side_rows(n):
        part = pl.ds(n * chunk, chunk)
        return [
            remote(tokens_ref.at[part], west_ref.at[part], side_send.at[0, n], side_recv.at[0, n], plan.east),
            remote(tokens_ref.at[part], east_ref.at[part], side_send.at[1, n], side_recv.at[1, n], plan.west),
        ]

    mine = cap_ref.at[plan.place, plan.side]
    theirs = cap_ref.at[plan.place, 1 - plan.side]
    sibling = remote(mine, mine, sib_send, sib_recv, plan.far)

    def ring(step, eastward):
        shift = count - (step - 1) if eastward else step - 1
        spot = cap_ref.at[lax.rem(plan.place + shift, count)]
        n = 0 if eastward else 1
        return remote(
            spot, spot, ring_send.at[n, step - 1], ring_recv.at[n, step - 1],
            plan.ring_east if eastward else plan.ring_west)

    def got(step, eastward):
        shift = count - step if eastward else step
        spot = cap_ref.at[lax.rem(plan.place + shift, count)]
        landed(spot, ring_recv.at[0 if eastward else 1, step - 1])

    def ring_on(step):
        @pl.when(plan.inner)
        def _():
            if step == 0:
                landed(mine, cap_recv)
                sibling.start()
            elif step == 1:
                landed(theirs, sib_recv)
            else:
                got(step - 1, True)
                if step - 1 <= west_steps:
                    got(step - 1, False)
            if 1 <= step <= east_steps:
                ring(step, True).start()
            if 1 <= step <= west_steps:
                ring(step, False).start()

    def take(tokens, slot):
        put_keys_values(
            tokens.reshape(2 * BLOCK, WIDTH), (slot, slot + 1), wide_ref, value_t_ref, k_ref, vt_ref)

    def attend_pairs(first, steps, columns):
        def body(t, carry):
            attend((first + 2 * t, first + 2 * t + 1), columns, mask_ref, k_ref, vt_ref, qd_ref, acc_ref)
            return carry

        lax.fori_loop(0, steps, body, 0)

    def finish(i):
        mixed_ref[i] = normalised(acc_ref, i)
        for p in range(PAIRS):
            hold_ref[0:1] = jnp.minimum(hold_ref[0:1], sums_hold(acc_ref[i, p, 96:97, :]))

    def take_sides(n):
        for copy in side_rows(n):
            copy.wait_recv()

        def body(t, carry):
            row = n * chunk + 2 * t
            take(west_ref[pl.ds(row, 2)], RADIUS + row)
            take(east_ref[pl.ds(row, 2)], 2 * FRAME + RADIUS + row)
            return carry

        lax.fori_loop(0, chunk // 2, body, 0)

    @pl.when(plan.at_pole)
    def _():
        for copy in gifts() + far_rows():
            copy.start()

    when_each(has, lambda n: lat_rows(n).start())
    for copy in side_rows(0):
        copy.start()

    def own(t, carry):
        tokens = tokens_ref[pl.ds(2 * t, 2)].reshape(2 * BLOCK, WIDTH)
        slot = FRAME + RADIUS + 2 * t
        put_keys_values(tokens, (slot, slot + 1), wide_ref, value_t_ref, k_ref, vt_ref)
        put_queries(tokens, (2 * t, 2 * t + 1), query_t_ref, qd_ref)
        return carry

    lax.fori_loop(0, ROWS // 2, own, 0)
    ring_on(0)
    for copy in side_rows(1):
        copy.start()
    attend_pairs(2, 2, (1,))
    ring_on(1)
    attend_pairs(6, 2, (1,))
    ring_on(2)
    for copy in side_rows(2):
        copy.start()
    when_each(lambda n: has(1 - n), lambda n: landed(halo_ref.at[pairs[n]], halo_recv.at[n]))

    @pl.when(plan.at_pole)
    def _():
        for n in range(RADIUS):
            landed(halo_ref.at[far_slot(n)], far_recv.at[n])

    corners = [
        remote(halo_ref, west_halo_ref, corner_send.at[0], corner_recv.at[0], plan.east),
        remote(halo_ref, east_halo_ref, corner_send.at[1], corner_recv.at[1], plan.west),
    ]
    for copy in corners:
        copy.start()

    def take_halo(column, which):
        take(halos_ref[which, 0:2], column * FRAME)
        take(halos_ref[which, 2:4], column * FRAME + ROWS + RADIUS)

    take_halo(1, 0)
    take_sides(0)
    ring_on(3)
    take_sides(1)
    attend_pairs(2, 2, (0, 2))
    ring_on(4)
    take_sides(2)
    keep = [
        pltpu.make_async_copy(west_ref, west_out, keep_sem.at[0]),
        pltpu.make_async_copy(east_ref, east_out, keep_sem.at[1]),
    ]
    for copy in keep:
        copy.start()
    attend_pairs(6, 2, (0, 2))
    ring_on(5)

    def send_part():
        return remote(part_ref, back_ref.at[plan.part], part_send, part_recv.at[plan.part], plan.pole)

    @pl.when(plan.inner)
    def _():
        landed(query_ref, query_recv)
        queries = jnp.concatenate([query_ref[...], query_ref[...]], axis=0)
        put_queries(queries, (0,), query_t_ref, cap_qd)

        def load(t, carry):
            tokens = cap_ref[t].reshape(2 * BLOCK, WIDTH)
            put_keys_values(tokens, (2 * t, 2 * t + 1), wide_ref, value_t_ref, cap_k, cap_vt)
            return carry

        lax.fori_loop(0, count, load, 0)
        attend_cap(2 * count, cap_k, cap_vt, cap_qd, cap_acc, cap_top)
        for p in range(PAIRS):
            part_ref[96 * p : 96 * p + 48] = cap_acc[p, 0:48, 0:128]
            part_ref[96 * p + 48 : 96 * p + 96] = cap_acc[p, 48:96, 128:256]
            for half in range(2):
                lanes = slice(128 * half, 128 * half + 128)
                n = 2 * p + half
                part_ref[WIDTH + n : WIDTH + n + 1] = cap_acc[p, 96:97, lanes]
                part_ref[WIDTH + HEADS + n : WIDTH + HEADS + n + 1] = cap_top[p, 0:1, lanes]
        send_part().start()

    def finish_row(t, carry):
        finish(2 + t)
        return carry

    lax.fori_loop(0, ROWS - 4, finish_row, 0)
    for copy in corners:
        copy.wait_recv()
    keep.append(pltpu.make_async_copy(halos_ref, halos_out, keep_sem.at[2]))
    keep[-1].start()
    take_halo(0, 1)
    take_halo(2, 2)

    def outer(t, carry):
        i = t + (ROWS - 4) * (t // 2)
        polar = jnp.logical_or(
            jnp.logical_and(plan.is_north, i == 0), jnp.logical_and(plan.is_south, i == ROWS - 1))

        @pl.when(jnp.logical_not(polar))
        def _():
            attend((i,), (0, 1, 2), mask_ref, k_ref, vt_ref, qd_ref, acc_ref)
            finish(i)

        return carry

    lax.fori_loop(0, 4, outer, 0)

    @pl.when(plan.at_pole)
    def _():
        row = jnp.where(plan.is_north, 0, ROWS - 1)
        counts = [0, 0, 0]
        for d in range(SPAN):
            north = d - RADIUS if d >= RADIUS else RADIUS - 1 - d
            south = RADIUS - d if d <= RADIUS else d - RADIUS - 1
            bit = mask_ref[row, d, 1].astype(F32)
            for r in range(3):
                hit = jnp.where(plan.is_north, float(north == r), float(south == r))
                counts[r] = counts[r] + bit * hit
        for r in range(3):
            landed(back_ref.at[r], part_recv.at[r])
        sums, tops = pl.ds(WIDTH, HEADS), pl.ds(WIDTH + HEADS, HEADS)
        used = [jnp.full((HEADS, BLOCK), n, F32) for n in counts]
        low = [jnp.where(used[r] > 0.5, back_ref[r, tops], -jnp.inf) for r in range(3)]
        top = jnp.maximum(jnp.maximum(low[0], low[1]), low[2])
        factors = [jnp.exp2(low[r] - top) * used[r] for r in range(3)]
        total = 1.0 / sum(factors[r] * back_ref[r, sums] for r in range(3))
        heads = []
        for h in range(HEADS):
            rows = pl.ds(HEAD_DIM * h, HEAD_DIM)
            heads.append(sum(factors[r][h : h + 1] * back_ref[r, rows] for r in range(3)) * total[h : h + 1])
        mixed_ref[row] = jnp.concatenate(heads, axis=0).astype(BF16)
        for copy in gifts() + far_rows():
            copy.wait_send()

    @pl.when(plan.inner)
    def _():
        sibling.wait_send()
        for step in range(1, east_steps + 1):
            ring(step, True).wait_send()
            if step <= west_steps:
                ring(step, False).wait_send()
        send_part().wait_send()

    when_each(has, lambda n: lat_rows(n).wait_send())
    for n in range(CHUNKS):
        for copy in side_rows(n):
            copy.wait_send()
    for copy in corners:
        copy.wait_send()
    for copy in keep:
        copy.wait()


def output_kernel(
    mask_ref, mixed_ref, hold_ref, w_out_ref, w_query_in, w_key_in, w_value_in, tokens_in, west_in, east_in, halos_in,
    out_ref,
    fixed_ref, strip_ref, weight_ref, k_ref, vt_ref, qd_ref, acc_ref, top_ref, wide_ref, query_t_ref, value_t_ref,
    list_ref, begin_ref, sem,
):
    lat = lax.axis_index("lat")
    last = lax.axis_size("lat") - 1

    def product(from_ref):
        def body(t, carry):
            both = jnp.concatenate([from_ref[2 * t], from_ref[2 * t + 1]], axis=1)
            result = dot(both, w_out_ref[...], ((0,), (0,))).astype(BF16)
            out_ref[pl.ds(2 * t, 2)] = result.reshape(2, BLOCK, WIDTH)
            return carry

        lax.fori_loop(0, ROWS // 2, body, 0, unroll=3)

    product(mixed_ref)
    holds = jnp.min(hold_ref[...]) > 0.5

    @pl.when(jnp.logical_not(holds))
    def _():
        def fetch(src, dst):
            copy = pltpu.make_async_copy(src, dst, sem)
            copy.start()
            copy.wait()

        fetch(w_key_in, weight_ref)
        prepare_keys(weight_ref, wide_ref)
        fetch(w_query_in, weight_ref)
        query_t_ref[...] = flipped(weight_ref)
        fetch(w_value_in, weight_ref)
        value_t_ref[...] = flipped(weight_ref)
        put_ones(vt_ref)
        qd_ref[...] = jnp.zeros_like(qd_ref)

        def take(src, slot):
            fetch(src, strip_ref)
            tokens = strip_ref[...].reshape(2 * BLOCK, WIDTH)
            put_keys_values(tokens, (slot, slot + 1), wide_ref, value_t_ref, k_ref, vt_ref)
            return tokens

        def load(t, carry):
            part = pl.ds(2 * t, 2)
            take(west_in.at[part], RADIUS + 2 * t)
            take(east_in.at[part], 2 * FRAME + RADIUS + 2 * t)
            tokens = take(tokens_in.at[part], FRAME + RADIUS + 2 * t)
            put_queries(tokens, (2 * t, 2 * t + 1), query_t_ref, qd_ref)
            return carry

        lax.fori_loop(0, ROWS // 2, load, 0)
        for column, which in ((1, 0), (0, 1), (2, 2)):
            take(halos_in.at[which, pl.ds(0, 2)], column * FRAME)
            take(halos_in.at[which, pl.ds(2, 2)], column * FRAME + ROWS + RADIUS)
        fixed_ref[...] = mixed_ref[...]

        def again(i, carry):
            pos = jnp.int32(0)
            for d in range(SPAN):
                for e in range(3):
                    list_ref[pos] = e * FRAME + i + d
                    pos = pos + (mask_ref[i, d, e] > 0).astype(jnp.int32)
            begin_ref[0] = pos
            polar = jnp.logical_or(
                jnp.logical_and(lat == 0, i == 0), jnp.logical_and(lat == last, i == ROWS - 1))

            @pl.when(jnp.logical_not(polar))
            def _():
                safe_row(
                    i, 0, 0, begin_ref[0], lambda n: list_ref[n], k_ref, vt_ref, qd_ref, acc_ref, top_ref)
                fixed_ref[i] = normalised(acc_ref, 0)

            return carry

        lax.fori_loop(0, ROWS, again, 0)
        product(fixed_ref)


def per_device(tokens, neighbor_mask, w_query, w_key, w_value, w_out):
    lon_count = lax.axis_size("lon")
    half = lon_count // 2
    strip = lambda *dims: jax.ShapeDtypeStruct((*dims, BLOCK, WIDTH), BF16)
    landing = lambda *dims: pltpu.VMEM((*dims, BLOCK, WIDTH), BF16)
    dma = pltpu.SemaphoreType.DMA
    keys = lambda n: pltpu.VMEM((n, BLOCK, LANES), BF16)
    values = lambda n: pltpu.VMEM((n, PAIRS, VROWS, BLOCK), BF16)
    queries = lambda n: pltpu.VMEM((n, PAIRS, 128, 256), BF16)
    square = pltpu.VMEM((WIDTH, WIDTH), BF16)
    wide = pltpu.VMEM((WIDTH, LANES), BF16)
    tops = pltpu.VMEM((PAIRS, 8, 256), F32)
    mixed = jax.ShapeDtypeStruct((ROWS, WIDTH, BLOCK), BF16)
    mixed, hold, west, east, halos = pl.pallas_call(
        grid_kernel,
        out_shape=[mixed, jax.ShapeDtypeStruct((8, 256), F32), strip(ROWS), strip(ROWS), strip(3, 4)],
        in_specs=[SMEM_SPEC] + [VMEM_SPEC] * 4,
        out_specs=[VMEM_SPEC] * 2 + [ANY_SPEC] * 3,
        scratch_shapes=[
            landing(ROWS), landing(ROWS), landing(3, 4), landing(), landing(half, 2),
            pltpu.VMEM((WIDTH + 2 * HEADS, BLOCK), F32),
            pltpu.VMEM((3, WIDTH + 2 * HEADS, BLOCK), F32),
            keys(SLOTS), values(SLOTS), queries(ROWS),
            pltpu.VMEM((ROWS, PAIRS, VROWS, 256), F32),
            keys(lon_count), values(lon_count), queries(1),
            pltpu.VMEM((PAIRS, VROWS, 256), F32),
            tops, wide, square, square,
            dma((2, CHUNKS)), dma((2, CHUNKS)), dma((2,)), dma((2,)), dma((2,)), dma((2,)), dma((2,)), dma((2,)),
            dma((6,)), dma, dma, dma, dma, dma((2, half // 2)), dma((2, half // 2)), dma, dma((3,)), dma((3,)),
        ],
        compiler_params=pltpu.CompilerParams(
            collective_id=0, has_side_effects=True, vmem_limit_bytes=VMEM_LIMIT),
        name="grid_attention",
    )(neighbor_mask, tokens, w_query, w_key, w_value)
    return pl.pallas_call(
        output_kernel,
        out_shape=strip(ROWS),
        in_specs=[SMEM_SPEC] + [VMEM_SPEC] * 3 + [ANY_SPEC] * 7,
        out_specs=VMEM_SPEC,
        scratch_shapes=[
            pltpu.VMEM((ROWS, WIDTH, BLOCK), BF16), landing(2), square,
            keys(SLOTS), values(SLOTS), queries(ROWS),
            pltpu.VMEM((1, PAIRS, VROWS, 256), F32),
            tops, wide, square, square,
            pltpu.SMEM((SPAN * 3 + 1,), jnp.int32), pltpu.SMEM((1,), jnp.int32), dma,
        ],
        compiler_params=pltpu.CompilerParams(vmem_limit_bytes=VMEM_LIMIT),
        name="output_product",
    )(neighbor_mask, mixed, hold, w_out, w_query, w_key, w_value, tokens, west, east, halos)


def solution(mesh):
    placed = (P("lat", "lon", None), P("lat", None, None), P(), P(), P(), P())
    return jax.shard_map(
        per_device, mesh=mesh, in_specs=placed, out_specs=P("lat", "lon", None), check_vma=False
    )
```

time: 547 us -> 226 us (0.41)
  Pallas kernels: 0 us -> 223 us
  matrix products: 166 us -> 0 us
  local copies, waits for them, and re-layouts: 143 us -> 1.44 us
  waiting for transfers between devices: 115 us -> 0 us
  other arithmetic: 53.8 us -> 0 us
  loops' own time: 38.3 us -> 0 us
  starting transfers between devices: 13.5 us -> 0 us
  between operations: 13.6 us -> 0.17 us
    pallas_call x0 -> x2, Pallas kernels: none -> 223 us  [the longest x1 155 us: per_device(): pl.pallas_call(output_kernel, out_shape=strip(ROWS), in_specs=[SMEM_SPEC]...]
    ppermute x6 -> x0, waiting for transfers between devices: 115 us -> none  [the longest x2 51.8 us: padded(): lax.ppermute(tail, axis, [(i, (i + 1) % count) for i in range(ends)])]
    dot_general x48 -> x0, matrix products: 91.2 us -> none  [the longest x12 43.7 us: attend(): jnp.einsum('hqk,khd->qhd', weights, head_values, preferred_element_type=j...]
    sub x12 -> x0, matrix products: 74.6 us -> none  [attend(): unscaled = counts[None, None, :] * jnp.exp(scores - highest)]
    dynamic_slice x64 -> x0, local copies, waits for them, and re-layouts: 61.4 us -> none  [the longest x12 24.3 us: one_row(): lax.dynamic_slice_in_dim(framed, row_index, span, 0)]
    slice x89 -> x0, local copies, waits for them, and re-layouts: 60.2 us -> none  [the longest x24 29.2 us: one_row(): window[:, :feat_width]]
    another operation x3 -> x0, loops' own time: 38.3 us -> none  [the longest x1 37.6 us: per_device(): attended = lax.map(one_row, jnp.arange(row_count))]
    add x16 -> x0, other arithmetic: 19.9 us -> none  [absorb(): new_sum = running_sum * factor + jnp.sum(unscaled, axis=-1)]
  transfers between devices with their start and end apart: 7 -> 0, of which waited for: 5 -> 0; matrix products, arithmetic and copies ran while one was open for 46% -> 0% of each run, Pallas kernels for 0% -> 0%
where the time goes in v4:
time: 226 us; the launch traced here: 225 us
  Pallas kernels  223 us (99%)
    pallas_call x1, Pallas kernels, per_device(): pl.pallas_call(output_kernel, out_shape=strip(ROWS), in_specs=[SMEM_SPEC]...  155 us
    pallas_call x1, Pallas kernels, per_device(): pl.pallas_call(grid_kernel, out_shape=[mixed, jax.ShapeDtypeStruct((8, 25...  68.8 us

profile of v4, /device:TPU:0, one launch (start us, length us, event | category | flops | bytes accessed | tf_op | source)
XLA Modules:
  0.0 225.1 jit_solution(10062937604903899142)
XLA Ops:
  0.0 1.4 copy.8.mask_ref
  1.4 68.8 %grid_attention.1 = (bf16[12,384,128]{2,1,0:T(8,128)(2,1)}, f32[8,256]{1,0:T(8,128)}, bf16[12,128,384]{2,1,0:T(8,128)(2,1)}, bf16[12,128,384]{2,1,0:T(8,128)(2,1)}, bf16[3,4,128,384]{3,2,1,0:T(8,128)(2,1)}) custom-call(s32[12,5,3]{2,1,0:T(8,128)} %copy.8.mask_ref, bf16[12,128,384]{2,1,0:T(8,128)(2,1)} %tokens_in.1, bf16[384,384]{1,0:T(8,128)(2,1)} %w_query_in.1, ...), custom_call_target="tpu_custom_call" | custom-call | tf_op jit(solution)/shard_map/grid_attention/pallas_call | solution.py:620
  70.3 154.6 %output_product.1 = bf16[12,128,384]{2,1,0:T(8,128)(2,1)} custom-call(s32[12,5,3]{2,1,0:T(8,128)} %copy.8.mask_ref, bf16[12,384,128]{2,1,0:T(8,128)(2,1)} %get-tuple-element.10.mixed_ref, f32[8,256]{1,0:T(8,128)} %get-tuple-element.11.hold_ref, bf16[384,384]{1,0:T(8,128)(2,1)} %w_out_ref.1, bf16[384,384]{1,0:T(8,128)(2,1)} %w_query_in.1, ...), custom_call_target="tpu_custom_call" | custom-call | tf_op jit(solution)/shard_map/output_product/pallas_call | solution.py:641

commit v5 on v4

--- a/solution.py
+++ b/solution.py
@@ -21,6 +21,7 @@
 LANES = 128 * PAIRS
 AHEAD = 8
 CHUNKS = 3
+OUTER_ROWS = (0, 1, ROWS - 2, ROWS - 1)
 SCORE_SCALE = HEAD_DIM ** -0.5 * 1.4426950408889634
 SUM_LOW = 1e-30
 SUM_HIGH = 1e30
@@ -46,22 +47,26 @@
     return ref[...].astype(F32).T.astype(BF16)
 
 
-def put_keys_values(tokens, slots, wide_ref, value_t_ref, k_ref, vt_ref):
-    keys = dot(tokens, wide_ref[...]).astype(BF16)
-    values = dot(value_t_ref[...], tokens, ((1,), (1,))).astype(BF16)
-    for n, slot in enumerate(slots):
-        k_ref[slot] = keys[128 * n : 128 * n + 128]
-        for p in range(PAIRS):
-            vt_ref[slot, p, 0:96] = values[96 * p : 96 * p + 96, 128 * n : 128 * n + 128]
-
-
-def put_queries(tokens, rows, query_t_ref, qd_ref):
-    queries = dot(query_t_ref[...], tokens, ((1,), (1,))).astype(BF16)
-    for n, row in enumerate(rows):
-        for p in range(PAIRS):
-            part = queries[96 * p : 96 * p + 96, 128 * n : 128 * n + 128]
-            qd_ref[row, p, 0:48, 0:128] = part[0:48]
-            qd_ref[row, p, 48:96, 128:256] = part[48:96]
+def put_tokens(strips, wide_ref, value_t_ref, k_ref, vt_ref):
+    keys = [dot(tokens, wide_ref[...]) for tokens, _ in strips]
+    values = [dot(value_t_ref[...], tokens, ((1,), (1,))) for tokens, _ in strips]
+    for (_, slot), key, value in zip(strips, keys, values):
+        key, value = key.astype(BF16), value.astype(BF16)
+        for n in range(2):
+            k_ref[slot + n] = key[128 * n : 128 * n + 128]
+            for p in range(PAIRS):
+                vt_ref[slot + n, p, 0:96] = value[96 * p : 96 * p + 96, 128 * n : 128 * n + 128]
+
+
+def put_queries(strips, query_t_ref, qd_ref):
+    queries = [dot(query_t_ref[...], tokens, ((1,), (1,))) for tokens, _ in strips]
+    for (_, rows), query in zip(strips, queries):
+        query = query.astype(BF16)
+        for n, row in enumerate(rows):
+            for p in range(PAIRS):
+                part = query[96 * p : 96 * p + 96, 128 * n : 128 * n + 128]
+                qd_ref[row, p, 0:48, 0:128] = part[0:48]
+                qd_ref[row, p, 48:96, 128:256] = part[48:96]
 
 
 def put_ones(vt_ref):
@@ -115,22 +120,20 @@
     return vt_ref[slot, p] * jnp.full((VROWS, BLOCK), bit, F32).astype(BF16)
 
 
-def attend(rows, columns, mask_ref, k_ref, vt_ref, qd_ref, acc_ref):
+def attend(work, fresh, mask_ref, k_ref, vt_ref, qd_ref, acc_ref):
     tiles = []
-    for i in rows:
-        blocks = [
-            (e * FRAME + i + d, mask_ref[i, d, e].astype(F32)) for e in columns for d in range(SPAN)
-        ]
-        tiles += [(i, blocks[n : n + 2]) for n in range(0, len(blocks), 2)]
-    chunks = [(i, tile, p) for i, tile in tiles for p in range(PAIRS)]
+    for i, blocks in work:
+        known = [(e * FRAME + i + d, mask_ref[i, d, e].astype(F32)) for d, e in blocks]
+        tiles += [(i, known[n : n + 2], fresh and n == 0) for n in range(0, len(known), 2)]
+    chunks = [(i, tile, p, begin) for i, tile, begin in tiles for p in range(PAIRS)]
 
     def scores(chunk):
-        i, tile, p = chunk
+        i, tile, p, _ = chunk
         keys = [k_ref[slot, :, 128 * p : 128 * p + 128] for slot, _ in tile]
         return dot(jnp.concatenate(keys, axis=0) if len(keys) > 1 else keys[0], qd_ref[i, p])
 
     def values(chunk, weights):
-        i, tile, p = chunk
+        i, tile, p, _ = chunk
         parts = [masked_values(vt_ref, slot, p, bit) for slot, bit in tile]
         return dot(jnp.concatenate(parts, axis=1) if len(parts) > 1 else parts[0], weights)
 
@@ -140,19 +143,23 @@
             held[step] = scores(chunks[step])
         if step >= AHEAD:
             chunk = chunks[step - AHEAD]
+            i, _, p, begin = chunk
             weights = jnp.exp2(held.pop(step - AHEAD) * SCORE_SCALE).astype(BF16)
-            acc_ref[chunk[0], chunk[2]] += values(chunk, weights)
+            if begin:
+                acc_ref[i, p] = values(chunk, weights)
+            else:
+                acc_ref[i, p] += values(chunk, weights)
 
 
 def attend_cap(blocks, k_ref, vt_ref, qd_ref, acc_ref, top_ref):
-    def scores(p):
-        qd = qd_ref[0, p]
+    def scores(q, p):
+        qd = qd_ref[q, p]
         return [
             dot(jnp.concatenate([k_ref[n + m, :, 128 * p : 128 * p + 128] for m in range(2)], axis=0), qd)
             for n in range(0, blocks, 2)
         ]
 
-    def finish(p, tiles):
+    def finish(q, p, tiles):
         tops = [jnp.max(tile, axis=0, keepdims=True) for tile in tiles]
         top = functools.reduce(jnp.maximum, tops) * SCORE_SCALE
         total = None
@@ -160,14 +167,16 @@
             weights = jnp.exp2(tile * SCORE_SCALE - top).astype(BF16)
             part = dot(jnp.concatenate([vt_ref[2 * n, p], vt_ref[2 * n + 1, p]], axis=1), weights)
             total = part if total is None else total + part
-        acc_ref[p] = total
-        top_ref[p, 0:1] = top
-
-    held = scores(0)
-    for p in range(PAIRS):
-        later = scores(p + 1) if p + 1 < PAIRS else None
-        finish(p, held)
-        held = later
+        acc_ref[q, p] = total
+        top_ref[q, p, 0:1] = top
+
+    turns = [(q, p) for p in range(PAIRS) for q in range(2)]
+    held = []
+    for n, turn in enumerate(turns + [None, None]):
+        if turn is not None:
+            held.append(scores(*turn))
+        if n >= 2:
+            finish(*turns[n - 2], held.pop(0))
 
 
 def at_device(lat, lon):
@@ -196,17 +205,24 @@
         self.east = (lat, lax.rem(lon + 1, self.lon_count))
         self.west = (lat, lax.rem(lon + self.lon_count - 1, self.lon_count))
         self.far = (lat, lax.rem(lon + half, self.lon_count))
-        self.place = lax.rem(lon, half)
         self.side = lon // half
-        base = lon - self.place
-        self.ring_east = (lat, base + lax.rem(self.place + 1, half))
-        self.ring_west = (lat, base + lax.rem(self.place + half - 1, half))
-        north_half = lat < (self.last + 1) // 2
-        self.pole = (jnp.where(north_half, 0, self.last), lon)
-        self.part = jnp.where(north_half, lat - 1, self.last - 1 - lat)
-
-    def helper(self, r):
-        return (jnp.where(self.is_north, 1 + r, self.last - 1 - r), self.lon)
+        self.y, self.core = lax.rem(lon, half) // 2, lax.rem(lon, 2)
+        self.y_count = half // 2
+        self.crosses_east, self.crosses_west = lax.rem(lon, half) == half - 1, lax.rem(lon, half) == 0
+        self.other_core = (lat, lon + 1 - 2 * self.core)
+        self.z_count = (self.last + 1) // 2
+        south = lax.rem(lat, 2)
+        self.pole = (jnp.where(south == 1, self.last, 0), lon)
+        away = jnp.where(south == 1, self.z_count - 1 - lat // 2, lat // 2)
+        self.part = jnp.where(away == 1, 0, jnp.where(away == 2, 2, 1))
+
+    def along_y(self, step):
+        y = lax.rem(self.y + step, self.y_count)
+        return (self.lat, self.side * self.half + 2 * y + self.core)
+
+    def helper(self, r, lon=None):
+        away = (1, self.z_count - 1, 2)[r]
+        return (jnp.where(self.is_north, 2 * away, self.last - 2 * away), self.lon if lon is None else lon)
 
     def cap_row(self, r):
         return jnp.where(self.is_north, r, ROWS - 1 - r)
@@ -229,21 +245,21 @@
     tell(plan.west)
     tell_if(lat < plan.last, [(lat + 1, lon)])
     tell_if(lat > 0, [(lat - 1, lon)])
-    tell_if(plan.at_pole, [plan.far] + [plan.helper(r) for r in range(3)])
-    tell_if(plan.inner, [plan.pole, plan.far, plan.ring_east, plan.ring_west])
+    tell_if(plan.at_pole, [plan.far] + [plan.helper(r, at) for r in range(3) for at in (lon, plan.far[1])])
+    tell_if(plan.inner, [plan.pole, plan.far, plan.other_core] + [plan.along_y(n) for n in (1, 2, 3)])
 
 
 def wait_receivers(plan):
-    pl.semaphore_wait(pltpu.get_barrier_semaphore(), jnp.where(plan.at_pole, 7, 8))
+    pl.semaphore_wait(pltpu.get_barrier_semaphore(), jnp.where(plan.at_pole, 7, 11))
 
 
 def grid_kernel(
     mask_ref, tokens_ref, w_query_ref, w_key_ref, w_value_ref,
     mixed_ref, hold_ref, west_out, east_out, halos_out,
-    west_ref, east_ref, halos_ref, query_ref, cap_ref, part_ref, back_ref,
+    west_ref, east_ref, halos_ref, query_ref, cap_ref, part_ref, stat_ref, back_ref, back_stat_ref,
     k_ref, vt_ref, qd_ref, acc_ref, cap_k, cap_vt, cap_qd, cap_acc, cap_top, wide_ref, query_t_ref, value_t_ref,
     side_send, side_recv, halo_send, halo_recv, far_send, far_recv, corner_send, corner_recv,
-    give_send, query_recv, cap_recv, sib_send, sib_recv, ring_send, ring_recv, part_send, part_recv, keep_sem,
+    give_send, query_recv, cap_recv, sib_send, sib_recv, y_send, y_recv, core_send, core_recv, part_send, part_recv, stat_send, stat_recv, keep_sem,
 ):
     plan = Plan()
     lat, last = plan.lat, plan.last
@@ -251,8 +267,7 @@
     pairs = (pl.ds(0, RADIUS), pl.ds(RADIUS, RADIUS))
     halo_ref, west_halo_ref, east_halo_ref = halos_ref.at[0], halos_ref.at[1], halos_ref.at[2]
     chunk = ROWS // CHUNKS
-    count = plan.half
-    east_steps, west_steps = count // 2, count // 2 - 1
+    y_count = plan.y_count
 
     tell_senders(plan)
     prepare_keys(w_key_ref, wide_ref)
@@ -262,18 +277,19 @@
     put_ones(cap_vt)
     qd_ref[...] = jnp.zeros_like(qd_ref)
     cap_qd[...] = jnp.zeros_like(cap_qd)
-    acc_ref[...] = jnp.zeros_like(acc_ref)
     hold_ref[...] = jnp.ones_like(hold_ref)
     wait_receivers(plan)
 
     def gifts():
-        copies = []
-        for r in range(3):
-            to = plan.helper(r)
-            copies.append(remote(
-                tokens_ref.at[plan.cap_row(r)], cap_ref.at[plan.place, plan.side], give_send.at[r], cap_recv, to))
-            copies.append(remote(tokens_ref.at[plan.cap_row(0)], query_ref, give_send.at[3 + r], query_recv, to))
-        return copies
+        keys = [
+            remote(tokens_ref.at[plan.cap_row(r)], cap_ref.at[plan.core, plan.y], give_send.at[r], cap_recv, plan.helper(r))
+            for r in range(3)
+        ]
+        queries = [
+            remote(tokens_ref.at[plan.cap_row(0)], query_ref.at[0], give_send.at[3 + r], query_recv, plan.helper(r))
+            for r in range(3)
+        ]
+        return keys + queries
 
     def far_slot(n):
         return jnp.where(plan.is_north, RADIUS - 1 - n, RADIUS + n)
@@ -305,50 +321,59 @@
             remote(tokens_ref.at[part], east_ref.at[part], side_send.at[1, n], side_recv.at[1, n], plan.west),
         ]
 
-    mine = cap_ref.at[plan.place, plan.side]
-    theirs = cap_ref.at[plan.place, 1 - plan.side]
-    sibling = remote(mine, mine, sib_send, sib_recv, plan.far)
-
-    def ring(step, eastward):
-        shift = count - (step - 1) if eastward else step - 1
-        spot = cap_ref.at[lax.rem(plan.place + shift, count)]
-        n = 0 if eastward else 1
-        return remote(
-            spot, spot, ring_send.at[n, step - 1], ring_recv.at[n, step - 1],
-            plan.ring_east if eastward else plan.ring_west)
-
-    def got(step, eastward):
-        shift = count - step if eastward else step
-        spot = cap_ref.at[lax.rem(plan.place + shift, count)]
-        landed(spot, ring_recv.at[0 if eastward else 1, step - 1])
-
-    def ring_on(step):
+    mine = cap_ref.at[plan.core, plan.y]
+    sibling = remote(query_ref.at[0], query_ref.at[1], sib_send, sib_recv, plan.far)
+
+    def along_y(step):
+        spot = cap_ref.at[plan.core, plan.y]
+        return remote(spot, spot, y_send.at[step], y_recv.at[step], plan.along_y(step))
+
+    def to_core(step):
+        spot = cap_ref.at[plan.core, lax.rem(plan.y + y_count - step, y_count)]
+        return remote(spot, spot, core_send.at[step], core_recv.at[step], plan.other_core)
+
+    def from_y(step):
+        landed(cap_ref.at[plan.core, lax.rem(plan.y + y_count - step, y_count)], y_recv.at[step])
+
+    def from_core(step):
+        landed(cap_ref.at[1 - plan.core, lax.rem(plan.y + y_count - step, y_count)], core_recv.at[step])
+
+    def cap_stage(stage):
         @pl.when(plan.inner)
         def _():
-            if step == 0:
+            if stage == 0:
                 landed(mine, cap_recv)
+                for step in range(1, y_count):
+                    along_y(step).start()
+                to_core(0).start()
+            if stage == 1:
+                landed(query_ref.at[0], query_recv)
                 sibling.start()
-            elif step == 1:
-                landed(theirs, sib_recv)
-            else:
-                got(step - 1, True)
-                if step - 1 <= west_steps:
-                    got(step - 1, False)
-            if 1 <= step <= east_steps:
-                ring(step, True).start()
-            if 1 <= step <= west_steps:
-                ring(step, False).start()
-
-    def take(tokens, slot):
-        put_keys_values(
-            tokens.reshape(2 * BLOCK, WIDTH), (slot, slot + 1), wide_ref, value_t_ref, k_ref, vt_ref)
-
-    def attend_pairs(first, steps, columns):
-        def body(t, carry):
-            attend((first + 2 * t, first + 2 * t + 1), columns, mask_ref, k_ref, vt_ref, qd_ref, acc_ref)
-            return carry
-
-        lax.fori_loop(0, steps, body, 0)
+            if stage == 2:
+                for step in range(1, y_count):
+                    from_y(step)
+                    to_core(step).start()
+            if stage == 3:
+                for step in range(y_count):
+                    from_core(step)
+                landed(query_ref.at[1], sib_recv)
+
+    def put(strips):
+        put_tokens([(tokens.reshape(2 * BLOCK, WIDTH), slot) for tokens, slot in strips], wide_ref, value_t_ref, k_ref, vt_ref)
+
+    def add(work, fresh=False):
+        attend(work, fresh, mask_ref, k_ref, vt_ref, qd_ref, acc_ref)
+
+    def add_rows(first, count, columns, fresh=False):
+        blocks = [(d, e) for e in columns for d in range(SPAN)]
+        add([(first + n, blocks) for n in range(count)], fresh)
+
+    def outer_work(columns, inside):
+        work = []
+        for i in OUTER_ROWS:
+            reach = [d for d in range(SPAN) if (0 <= i + d - RADIUS < ROWS) == inside]
+            work.append((i, [(d, e) for e in columns for d in reach]))
+        return work
 
     def finish(i):
         mixed_ref[i] = normalised(acc_ref, i)
@@ -358,14 +383,15 @@
     def take_sides(n):
         for copy in side_rows(n):
             copy.wait_recv()
-
-        def body(t, carry):
-            row = n * chunk + 2 * t
-            take(west_ref[pl.ds(row, 2)], RADIUS + row)
-            take(east_ref[pl.ds(row, 2)], 2 * FRAME + RADIUS + row)
-            return carry
-
-        lax.fori_loop(0, chunk // 2, body, 0)
+        strips = []
+        for row in range(n * chunk, n * chunk + chunk, 2):
+            strips.append((west_ref[row : row + 2], RADIUS + row))
+            strips.append((east_ref[row : row + 2], 2 * FRAME + RADIUS + row))
+        put(strips)
+
+    def halo_strips(column, which):
+        return [
+            (halos_ref[which, 0:2], column * FRAME), (halos_ref[which, 2:4], column * FRAME + ROWS + RADIUS)]
 
     @pl.when(plan.at_pole)
     def _():
@@ -373,26 +399,33 @@
             copy.start()
 
     when_each(has, lambda n: lat_rows(n).start())
-    for copy in side_rows(0):
-        copy.start()
+    crossing = (plan.crosses_east, plan.crosses_west)
+    for n in range(CHUNKS):
+        for copy, crosses in zip(side_rows(n), crossing):
+            pl.when(jnp.logical_or(crosses, n == 0))(copy.start)
+
+    def start_others(n):
+        for copy, crosses in zip(side_rows(n), crossing):
+            pl.when(jnp.logical_not(crosses))(copy.start)
 
     def own(t, carry):
-        tokens = tokens_ref[pl.ds(2 * t, 2)].reshape(2 * BLOCK, WIDTH)
-        slot = FRAME + RADIUS + 2 * t
-        put_keys_values(tokens, (slot, slot + 1), wide_ref, value_t_ref, k_ref, vt_ref)
-        put_queries(tokens, (2 * t, 2 * t + 1), query_t_ref, qd_ref)
+        first = [4 * t, 4 * t + 2]
+        strips = [tokens_ref[pl.ds(n, 2)] for n in first]
+        put([(tokens, FRAME + RADIUS + n) for tokens, n in zip(strips, first)])
+        put_queries(
+            [(tokens.reshape(2 * BLOCK, WIDTH), (n, n + 1)) for tokens, n in zip(strips, first)], query_t_ref, qd_ref)
         return carry
 
-    lax.fori_loop(0, ROWS // 2, own, 0)
-    ring_on(0)
-    for copy in side_rows(1):
-        copy.start()
-    attend_pairs(2, 2, (1,))
-    ring_on(1)
-    attend_pairs(6, 2, (1,))
-    ring_on(2)
-    for copy in side_rows(2):
-        copy.start()
+    lax.fori_loop(0, ROWS // 4, own, 0)
+    cap_stage(0)
+    add_rows(2, 4, (1,), True)
+    cap_stage(1)
+    start_others(1)
+    add_rows(6, 4, (1,), True)
+    start_others(2)
+    add(outer_work((1,), True), True)
+    take_sides(0)
+    cap_stage(2)
     when_each(lambda n: has(1 - n), lambda n: landed(halo_ref.at[pairs[n]], halo_recv.at[n]))
 
     @pl.when(plan.at_pole)
@@ -406,17 +439,41 @@
     ]
     for copy in corners:
         copy.start()
-
-    def take_halo(column, which):
-        take(halos_ref[which, 0:2], column * FRAME)
-        take(halos_ref[which, 2:4], column * FRAME + ROWS + RADIUS)
-
-    take_halo(1, 0)
-    take_sides(0)
-    ring_on(3)
+    put(halo_strips(1, 0))
     take_sides(1)
-    attend_pairs(2, 2, (0, 2))
-    ring_on(4)
+    add_rows(2, 4, (0, 2))
+    cap_stage(3)
+
+    def send_parts():
+        copies = []
+        for q, to in enumerate((plan.pole, (plan.pole[0], plan.far[1]))):
+            copies.append(remote(
+                part_ref.at[q], back_ref.at[plan.part, q], part_send.at[q], part_recv.at[plan.part, q], to))
+            copies.append(remote(
+                stat_ref.at[q], back_stat_ref.at[plan.part, q], stat_send.at[q], stat_recv.at[plan.part, q], to))
+        return copies
+
+    @pl.when(plan.inner)
+    def _():
+        put_queries([(query_ref[...].reshape(2 * BLOCK, WIDTH), (0, 1))], query_t_ref, cap_qd)
+        strips = [
+            (cap_ref[core].reshape(y_count // 2, 2 * BLOCK, WIDTH)[n], core * y_count + 2 * n)
+            for core in range(2) for n in range(y_count // 2)
+        ]
+        put_tokens(strips, wide_ref, value_t_ref, cap_k, cap_vt)
+        attend_cap(2 * y_count, cap_k, cap_vt, cap_qd, cap_acc, cap_top)
+        for q in range(2):
+            for p in range(PAIRS):
+                part_ref[q, 96 * p : 96 * p + 48] = cap_acc[q, p, 0:48, 0:128].astype(BF16)
+                part_ref[q, 96 * p + 48 : 96 * p + 96] = cap_acc[q, p, 48:96, 128:256].astype(BF16)
+                for half in range(2):
+                    lanes = slice(128 * half, 128 * half + 128)
+                    n = 2 * p + half
+                    stat_ref[q, n : n + 1] = cap_acc[q, p, 96:97, lanes]
+                    stat_ref[q, HEADS + n : HEADS + n + 1] = cap_top[q, p, 0:1, lanes]
+        for copy in send_parts():
+            copy.start()
+
     take_sides(2)
     keep = [
         pltpu.make_async_copy(west_ref, west_out, keep_sem.at[0]),
@@ -424,34 +481,9 @@
     ]
     for copy in keep:
         copy.start()
-    attend_pairs(6, 2, (0, 2))
-    ring_on(5)
-
-    def send_part():
-        return remote(part_ref, back_ref.at[plan.part], part_send, part_recv.at[plan.part], plan.pole)
-
-    @pl.when(plan.inner)
-    def _():
-        landed(query_ref, query_recv)
-        queries = jnp.concatenate([query_ref[...], query_ref[...]], axis=0)
-        put_queries(queries, (0,), query_t_ref, cap_qd)
-
-        def load(t, carry):
-            tokens = cap_ref[t].reshape(2 * BLOCK, WIDTH)
-            put_keys_values(tokens, (2 * t, 2 * t + 1), wide_ref, value_t_ref, cap_k, cap_vt)
-            return carry
-
-        lax.fori_loop(0, count, load, 0)
-        attend_cap(2 * count, cap_k, cap_vt, cap_qd, cap_acc, cap_top)
-        for p in range(PAIRS):
-            part_ref[96 * p : 96 * p + 48] = cap_acc[p, 0:48, 0:128]
-            part_ref[96 * p + 48 : 96 * p + 96] = cap_acc[p, 48:96, 128:256]
-            for half in range(2):
-                lanes = slice(128 * half, 128 * half + 128)
-                n = 2 * p + half
-                part_ref[WIDTH + n : WIDTH + n + 1] = cap_acc[p, 96:97, lanes]
-                part_ref[WIDTH + HEADS + n : WIDTH + HEADS + n + 1] = cap_top[p, 0:1, lanes]
-        send_part().start()
+    add_rows(6, 4, (0, 2))
+    add(outer_work((0, 2), True))
+    add(outer_work((1,), False))
 
     def finish_row(t, carry):
         finish(2 + t)
@@ -462,22 +494,10 @@
         copy.wait_recv()
     keep.append(pltpu.make_async_copy(halos_ref, halos_out, keep_sem.at[2]))
     keep[-1].start()
-    take_halo(0, 1)
-    take_halo(2, 2)
-
-    def outer(t, carry):
-        i = t + (ROWS - 4) * (t // 2)
-        polar = jnp.logical_or(
-            jnp.logical_and(plan.is_north, i == 0), jnp.logical_and(plan.is_south, i == ROWS - 1))
-
-        @pl.when(jnp.logical_not(polar))
-        def _():
-            attend((i,), (0, 1, 2), mask_ref, k_ref, vt_ref, qd_ref, acc_ref)
-            finish(i)
-
-        return carry
-
-    lax.fori_loop(0, 4, outer, 0)
+    put(halo_strips(0, 1) + halo_strips(2, 2))
+    add(outer_work((0, 2), False))
+    for i in OUTER_ROWS:
+        finish(i)
 
     @pl.when(plan.at_pole)
     def _():
@@ -490,18 +510,22 @@
             for r in range(3):
                 hit = jnp.where(plan.is_north, float(north == r), float(south == r))
                 counts[r] = counts[r] + bit * hit
-        for r in range(3):
-            landed(back_ref.at[r], part_recv.at[r])
-        sums, tops = pl.ds(WIDTH, HEADS), pl.ds(WIDTH + HEADS, HEADS)
-        used = [jnp.full((HEADS, BLOCK), n, F32) for n in counts]
-        low = [jnp.where(used[r] > 0.5, back_ref[r, tops], -jnp.inf) for r in range(3)]
-        top = jnp.maximum(jnp.maximum(low[0], low[1]), low[2])
-        factors = [jnp.exp2(low[r] - top) * used[r] for r in range(3)]
-        total = 1.0 / sum(factors[r] * back_ref[r, sums] for r in range(3))
+        parts = [(r, q) for r in range(3) for q in range(2)]
+        for r, q in parts:
+            landed(back_stat_ref.at[r, q], stat_recv.at[r, q])
+            landed(back_ref.at[r, q], part_recv.at[r, q])
+        sums, tops = pl.ds(0, HEADS), pl.ds(HEADS, HEADS)
+        used = [jnp.full((HEADS, BLOCK), counts[r], F32) for r, _ in parts]
+        low = [jnp.where(n > 0.5, back_stat_ref[r, q, tops], -jnp.inf) for n, (r, q) in zip(used, parts)]
+        top = functools.reduce(jnp.maximum, low)
+        factors = [jnp.exp2(t - top) * n for t, n in zip(low, used)]
+        total = 1.0 / sum(f * back_stat_ref[r, q, sums] for f, (r, q) in zip(factors, parts))
         heads = []
         for h in range(HEADS):
             rows = pl.ds(HEAD_DIM * h, HEAD_DIM)
-            heads.append(sum(factors[r][h : h + 1] * back_ref[r, rows] for r in range(3)) * total[h : h + 1])
+            heads.append(
+                sum(f[h : h + 1] * back_ref[r, q, rows].astype(F32) for f, (r, q) in zip(factors, parts))
+                * total[h : h + 1])
         mixed_ref[row] = jnp.concatenate(heads, axis=0).astype(BF16)
         for copy in gifts() + far_rows():
             copy.wait_send()
@@ -509,11 +533,12 @@
     @pl.when(plan.inner)
     def _():
         sibling.wait_send()
-        for step in range(1, east_steps + 1):
-            ring(step, True).wait_send()
-            if step <= west_steps:
-                ring(step, False).wait_send()
-        send_part().wait_send()
+        for step in range(y_count):
+            to_core(step).wait_send()
+            if step > 0:
+                along_y(step).wait_send()
+        for copy in send_parts():
+            copy.wait_send()
 
     when_each(has, lambda n: lat_rows(n).wait_send())
     for n in range(CHUNKS):
@@ -565,7 +590,7 @@
         def take(src, slot):
             fetch(src, strip_ref)
             tokens = strip_ref[...].reshape(2 * BLOCK, WIDTH)
-            put_keys_values(tokens, (slot, slot + 1), wide_ref, value_t_ref, k_ref, vt_ref)
+            put_tokens([(tokens, slot)], wide_ref, value_t_ref, k_ref, vt_ref)
             return tokens
 
         def load(t, carry):
@@ -573,7 +598,7 @@
             take(west_in.at[part], RADIUS + 2 * t)
             take(east_in.at[part], 2 * FRAME + RADIUS + 2 * t)
             tokens = take(tokens_in.at[part], FRAME + RADIUS + 2 * t)
-            put_queries(tokens, (2 * t, 2 * t + 1), query_t_ref, qd_ref)
+            put_queries([(tokens, (2 * t, 2 * t + 1))], query_t_ref, qd_ref)
             return carry
 
         lax.fori_loop(0, ROWS // 2, load, 0)
@@ -623,16 +648,17 @@
         in_specs=[SMEM_SPEC] + [VMEM_SPEC] * 4,
         out_specs=[VMEM_SPEC] * 2 + [ANY_SPEC] * 3,
         scratch_shapes=[
-            landing(ROWS), landing(ROWS), landing(3, 4), landing(), landing(half, 2),
-            pltpu.VMEM((WIDTH + 2 * HEADS, BLOCK), F32),
-            pltpu.VMEM((3, WIDTH + 2 * HEADS, BLOCK), F32),
+            landing(ROWS), landing(ROWS), landing(3, 4), landing(2), landing(2, half // 2),
+            pltpu.VMEM((2, WIDTH, BLOCK), BF16), pltpu.VMEM((2, 2 * HEADS, BLOCK), F32),
+            pltpu.VMEM((3, 2, WIDTH, BLOCK), BF16), pltpu.VMEM((3, 2, 2 * HEADS, BLOCK), F32),
             keys(SLOTS), values(SLOTS), queries(ROWS),
             pltpu.VMEM((ROWS, PAIRS, VROWS, 256), F32),
-            keys(lon_count), values(lon_count), queries(1),
-            pltpu.VMEM((PAIRS, VROWS, 256), F32),
-            tops, wide, square, square,
+            keys(half), values(half), queries(2),
+            pltpu.VMEM((2, PAIRS, VROWS, 256), F32), pltpu.VMEM((2, PAIRS, 8, 256), F32),
+            wide, square, square,
             dma((2, CHUNKS)), dma((2, CHUNKS)), dma((2,)), dma((2,)), dma((2,)), dma((2,)), dma((2,)), dma((2,)),
-            dma((6,)), dma, dma, dma, dma, dma((2, half // 2)), dma((2, half // 2)), dma, dma((3,)), dma((3,)),
+            dma((6,)), dma, dma, dma, dma, *[dma((half // 2,))] * 4,
+            dma((2,)), dma((3, 2)), dma((2,)), dma((3, 2)), dma((3,)),
         ],
         compiler_params=pltpu.CompilerParams(
             collective_id=0, has_side_effects=True, vmem_limit_bytes=VMEM_LIMIT),

time: 226 us -> 221 us (0.978)
  Pallas kernels: 223 us -> 218 us
    pallas_call x1, Pallas kernels: 68.8 us -> 56.6 us  [per_device(): pl.pallas_call(grid_kernel, out_shape=[mixed, jax.ShapeDtypeStruct((8, 25...]
    pallas_call x1, Pallas kernels: 155 us -> 161 us  [per_device(): pl.pallas_call(output_kernel, out_shape=strip(ROWS), in_specs=[SMEM_SPEC]...]
where the time goes in v5:
time: 221 us; the launch traced here: 220 us
  Pallas kernels  218 us (99%)
    pallas_call x1, Pallas kernels, per_device(): pl.pallas_call(output_kernel, out_shape=strip(ROWS), in_specs=[SMEM_SPEC]...  161 us
    pallas_call x1, Pallas kernels, per_device(): pl.pallas_call(grid_kernel, out_shape=[mixed, jax.ShapeDtypeStruct((8, 25...  56.6 us

profile of v5, /device:TPU:0, one launch (start us, length us, event | category | flops | bytes accessed | tf_op | source)
XLA Modules:
  0.0 219.7 jit_solution(13943177035931629655)
XLA Ops:
  0.0 1.4 copy.8.mask_ref
  1.4 56.6 %grid_attention.1 = (bf16[12,384,128]{2,1,0:T(8,128)(2,1)}, f32[8,256]{1,0:T(8,128)}, bf16[12,128,384]{2,1,0:T(8,128)(2,1)}, bf16[12,128,384]{2,1,0:T(8,128)(2,1)}, bf16[3,4,128,384]{3,2,1,0:T(8,128)(2,1)}) custom-call(s32[12,5,3]{2,1,0:T(8,128)} %copy.8.mask_ref, bf16[12,128,384]{2,1,0:T(8,128)(2,1)} %tokens_in.1, bf16[384,384]{1,0:T(8,128)(2,1)} %w_query_in.1, ...), custom_call_target="tpu_custom_call" | custom-call | tf_op jit(solution)/shard_map/grid_attention/pallas_call | solution.py:645
  58.0 161.5 %output_product.1 = bf16[12,128,384]{2,1,0:T(8,128)(2,1)} custom-call(s32[12,5,3]{2,1,0:T(8,128)} %copy.8.mask_ref, bf16[12,384,128]{2,1,0:T(8,128)(2,1)} %get-tuple-element.10.mixed_ref, f32[8,256]{1,0:T(8,128)} %get-tuple-element.11.hold_ref, bf16[384,384]{1,0:T(8,128)(2,1)} %w_out_ref.1, bf16[384,384]{1,0:T(8,128)(2,1)} %w_query_in.1, ...), custom_call_target="tpu_custom_call" | custom-call | tf_op jit(solution)/shard_map/output_product/pallas_call | solution.py:667

commit v6 on v5

--- a/solution.py
+++ b/solution.py
@@ -208,7 +208,6 @@
         self.side = lon // half
         self.y, self.core = lax.rem(lon, half) // 2, lax.rem(lon, 2)
         self.y_count = half // 2
-        self.crosses_east, self.crosses_west = lax.rem(lon, half) == half - 1, lax.rem(lon, half) == 0
         self.other_core = (lat, lon + 1 - 2 * self.core)
         self.z_count = (self.last + 1) // 2
         south = lax.rem(lat, 2)
@@ -287,9 +286,9 @@
         ]
         queries = [
             remote(tokens_ref.at[plan.cap_row(0)], query_ref.at[0], give_send.at[3 + r], query_recv, plan.helper(r))
-            for r in range(3)
+            for r in range(1, 3)
         ]
-        return keys + queries
+        return [keys[2], queries[1], keys[1], queries[0], keys[0]]
 
     def far_slot(n):
         return jnp.where(plan.is_north, RADIUS - 1 - n, RADIUS + n)
@@ -347,7 +346,14 @@
                     along_y(step).start()
                 to_core(0).start()
             if stage == 1:
-                landed(query_ref.at[0], query_recv)
+                @pl.when(plan.part > 0)
+                def _():
+                    landed(query_ref.at[0], query_recv)
+
+                @pl.when(plan.part == 0)
+                def _():
+                    query_ref[0] = mine[...]
+
                 sibling.start()
             if stage == 2:
                 for step in range(1, y_count):
@@ -393,20 +399,18 @@
         return [
             (halos_ref[which, 0:2], column * FRAME), (halos_ref[which, 2:4], column * FRAME + ROWS + RADIUS)]
 
+    when_each(has, lambda n: lat_rows(n).start())
+
     @pl.when(plan.at_pole)
     def _():
-        for copy in gifts() + far_rows():
+        for copy in far_rows() + gifts():
             copy.start()
 
-    when_each(has, lambda n: lat_rows(n).start())
-    crossing = (plan.crosses_east, plan.crosses_west)
-    for n in range(CHUNKS):
-        for copy, crosses in zip(side_rows(n), crossing):
-            pl.when(jnp.logical_or(crosses, n == 0))(copy.start)
-
-    def start_others(n):
-        for copy, crosses in zip(side_rows(n), crossing):
-            pl.when(jnp.logical_not(crosses))(copy.start)
+    def start_sides(n):
+        for copy in side_rows(n):
+            copy.start()
+
+    start_sides(0)
 
     def own(t, carry):
         first = [4 * t, 4 * t + 2]
@@ -418,14 +422,14 @@
 
     lax.fori_loop(0, ROWS // 4, own, 0)
     cap_stage(0)
+    start_sides(1)
     add_rows(2, 4, (1,), True)
     cap_stage(1)
-    start_others(1)
     add_rows(6, 4, (1,), True)
-    start_others(2)
+    start_sides(2)
     add(outer_work((1,), True), True)
+    cap_stage(2)
     take_sides(0)
-    cap_stage(2)
     when_each(lambda n: has(1 - n), lambda n: landed(halo_ref.at[pairs[n]], halo_recv.at[n]))
 
     @pl.when(plan.at_pole)
@@ -440,8 +444,7 @@
     for copy in corners:
         copy.start()
     put(halo_strips(1, 0))
-    take_sides(1)
-    add_rows(2, 4, (0, 2))
+    add(outer_work((1,), False))
     cap_stage(3)
 
     def send_parts():
@@ -474,6 +477,8 @@
         for copy in send_parts():
             copy.start()
 
+    take_sides(1)
+    add_rows(2, 4, (0, 2))
     take_sides(2)
     keep = [
         pltpu.make_async_copy(west_ref, west_out, keep_sem.at[0]),
@@ -483,7 +488,6 @@
         copy.start()
     add_rows(6, 4, (0, 2))
     add(outer_work((0, 2), True))
-    add(outer_work((1,), False))
 
     def finish_row(t, carry):
         finish(2 + t)

time: 221 us -> 212 us (0.959)
  the two profiles are of different devices: /device:TPU:0 before, /device:TPU:1 now
where the time goes in v6:
time: 212 us; the launch traced here: 208 us
  Pallas kernels  206 us (97%)
    pallas_call x1, Pallas kernels, per_device(): pl.pallas_call(output_kernel, out_shape=strip(ROWS), in_specs=[SMEM_SPEC]...  157 us
    pallas_call x1, Pallas kernels, per_device(): pl.pallas_call(grid_kernel, out_shape=[mixed, jax.ShapeDtypeStruct((8, 25...  49.4 us

profile of v6, /device:TPU:1, one launch (start us, length us, event | category | flops | bytes accessed | tf_op | source)
XLA Modules:
  0.0 207.9 jit_solution(2763083198178812865)
XLA Ops:
  0.0 1.4 copy.8.mask_ref
  1.4 49.4 %grid_attention.1 = (bf16[12,384,128]{2,1,0:T(8,128)(2,1)}, f32[8,256]{1,0:T(8,128)}, bf16[12,128,384]{2,1,0:T(8,128)(2,1)}, bf16[12,128,384]{2,1,0:T(8,128)(2,1)}, bf16[3,4,128,384]{3,2,1,0:T(8,128)(2,1)}) custom-call(s32[12,5,3]{2,1,0:T(8,128)} %copy.8.mask_ref, bf16[12,128,384]{2,1,0:T(8,128)(2,1)} %tokens_in.1, bf16[384,384]{1,0:T(8,128)(2,1)} %w_query_in.1, ...), custom_call_target="tpu_custom_call" | custom-call | tf_op jit(solution)/shard_map/grid_attention/pallas_call | solution.py:649
  50.9 156.8 %output_product.1 = bf16[12,128,384]{2,1,0:T(8,128)(2,1)} custom-call(s32[12,5,3]{2,1,0:T(8,128)} %copy.8.mask_ref, bf16[12,384,128]{2,1,0:T(8,128)(2,1)} %get-tuple-element.10.mixed_ref, f32[8,256]{1,0:T(8,128)} %get-tuple-element.11.hold_ref, bf16[384,384]{1,0:T(8,128)(2,1)} %w_out_ref.1, bf16[384,384]{1,0:T(8,128)(2,1)} %w_query_in.1, ...), custom_call_target="tpu_custom_call" | custom-call | tf_op jit(solution)/shard_map/output_product/pallas_call | solution.py:671

commit v7 on v6

--- a/solution.py
+++ b/solution.py
@@ -288,7 +288,7 @@
             remote(tokens_ref.at[plan.cap_row(0)], query_ref.at[0], give_send.at[3 + r], query_recv, plan.helper(r))
             for r in range(1, 3)
         ]
-        return [keys[2], queries[1], keys[1], queries[0], keys[0]]
+        return [keys[2], queries[1], keys[0], keys[1], queries[0]]
 
     def far_slot(n):
         return jnp.where(plan.is_north, RADIUS - 1 - n, RADIUS + n)

time: 212 us -> 213 us (level)
  the two profiles are of different devices: /device:TPU:1 before, /device:TPU:0 now
where the time goes in v7:
time: 213 us; the launch traced here: 210 us
  Pallas kernels  208 us (98%)
    pallas_call x1, Pallas kernels, per_device(): pl.pallas_call(output_kernel, out_shape=strip(ROWS), in_specs=[SMEM_SPEC]...  159 us
    pallas_call x1, Pallas kernels, per_device(): pl.pallas_call(grid_kernel, out_shape=[mixed, jax.ShapeDtypeStruct((8, 25...  49 us

profile of v7, /device:TPU:0, one launch (start us, length us, event | category | flops | bytes accessed | tf_op | source)
XLA Modules:
  0.0 209.7 jit_solution(6297755517367255846)
XLA Ops:
  0.0 1.4 copy.8.mask_ref
  1.4 49.0 %grid_attention.1 = (bf16[12,384,128]{2,1,0:T(8,128)(2,1)}, f32[8,256]{1,0:T(8,128)}, bf16[12,128,384]{2,1,0:T(8,128)(2,1)}, bf16[12,128,384]{2,1,0:T(8,128)(2,1)}, bf16[3,4,128,384]{3,2,1,0:T(8,128)(2,1)}) custom-call(s32[12,5,3]{2,1,0:T(8,128)} %copy.8.mask_ref, bf16[12,128,384]{2,1,0:T(8,128)(2,1)} %tokens_in.1, bf16[384,384]{1,0:T(8,128)(2,1)} %w_query_in.1, ...), custom_call_target="tpu_custom_call" | custom-call | tf_op jit(solution)/shard_map/grid_attention/pallas_call | solution.py:649
  50.5 159.0 %output_product.1 = bf16[12,128,384]{2,1,0:T(8,128)(2,1)} custom-call(s32[12,5,3]{2,1,0:T(8,128)} %copy.8.mask_ref, bf16[12,384,128]{2,1,0:T(8,128)(2,1)} %get-tuple-element.10.mixed_ref, f32[8,256]{1,0:T(8,128)} %get-tuple-element.11.hold_ref, bf16[384,384]{1,0:T(8,128)(2,1)} %w_out_ref.1, bf16[384,384]{1,0:T(8,128)(2,1)} %w_query_in.1, ...), custom_call_target="tpu_custom_call" | custom-call | tf_op jit(solution)/shard_map/output_product/pallas_call | solution.py:671
